TPU v7x, 256 devices: a whole 4x4x8 slice. The times are simulated.
256 devices in a mesh: dp: 16 (over z, core), ep: 16 (over y, x).
Axes of the slice: x: 4, y: 4, z: 8, core: 2. Of those that a mesh axis runs over, the one named last changes fastest.
Arguments:
- latent_cache: bfloat16 [64, 8192, 576], P('dp', 'ep'), may hold values from -6 to 6, as said below
- lengths: int32 [64], replicated, may hold values from 2 to 8192, as said below
- queries: bfloat16 [2, 64, 128, 576], P(None, 'dp'), may hold values from -12 to 12
- fresh_latent: bfloat16 [2, 64, 576], P(None, 'dp'), may hold values from -6 to 6
- leaving: int32 [16], replicated, may hold values from 0 to 3
- target: int32 [16], replicated, may hold values from 0 to 15, as said below
- value_weight: bfloat16 [128, 512, 128], P('ep'), may hold values from -0.25 to 0.25
- output_weight: bfloat16 [128, 128, 7168], P('ep', 'dp'), may hold values from -0.0625 to 0.0625
- residual_stream: bfloat16 [2, 64, 7168], replicated, may hold values from -17 to 17
- norm_gain: bfloat16 [7168], replicated, may hold values from 0.099609375 to 1.8984375
- expert_ids: int32 [2, 64, 8], replicated, may hold values from 0 to 15, all different within a row
- gate_codes: int32 [2, 64, 8], replicated, may hold values from 1 to 65535
- gate_weight: bfloat16 [16, 7168, 2048], P('ep', None, 'dp'), may hold values from -0.0625 to 0.0625
- up_weight: bfloat16 [16, 7168, 2048], P('ep', None, 'dp'), may hold values from -0.0625 to 0.0625
- down_weight: bfloat16 [16, 2048, 7168], P('ep', 'dp'), may hold values from -0.1875 to 0.1875
Outputs:
- mixed: bfloat16 [2, 64, 7168], P(None, 'dp', 'ep')
Inputs may be any that keep to these rules, and one draw needn't show every extreme that they name: `latent_cache`: entries at positions at or beyond a slot's length are never read. `lengths`: one session has exactly 8192 cached positions. A permutation of the ranks without a fixed point: rank r hands the session of slot leaving[r] to rank target[r], which puts it in its own slot leaving[target[r]].
All inputs are finite; a program needn't handle non-finite values.
Results may differ from a plain program's by a relative error of at most 0.015.
Values may be sent and summed in bfloat16 or wider, within the bound.
A program may use at most 128 MiB of HBM per device.

v0:
```python
import jax
import jax.numpy as jnp
from jax import lax
from jax.sharding import PartitionSpec as P

LAT = 512


SCORE_SCALE = 192.0 ** (-0.5)
ROUTE_SCALE = 2.5
NORM_EPS = 1e-06
MASKED = -1e30


def combined_all(value, axis, combine):
    everything = jax.tree.map(lambda part: lax.all_gather(part, axis), value)
    first = jax.tree.map(lambda part: part[0], everything)

    def hop(k, so_far):
        return combine(so_far, jax.tree.map(lambda part: part[k], everything))

    return lax.fori_loop(1, lax.axis_size(axis), hop, first)


def session_order(leaving, target, slot_count):
    rank_count = leaving.shape[0]
    positions = jnp.arange(rank_count * slot_count, dtype=jnp.int32)
    arrive = target * slot_count + leaving[target]
    depart = jnp.arange(rank_count, dtype=jnp.int32) * slot_count + leaving
    return positions.at[arrive].set(depart)


def combine_partial(earlier, later):
    peak_early, sum_early, values_early = earlier
    peak_late, sum_late, values_late = later
    best_score = jnp.maximum(peak_early, peak_late)
    scale_early = jnp.exp(peak_early - best_score)
    scale_late = jnp.exp(peak_late - best_score)
    merged_sum = scale_early * sum_early + scale_late * sum_late
    merged_values = scale_early[..., None] * values_early + scale_late[..., None] * values_late
    return (best_score, merged_sum, merged_values)


def attend_local(query_rows, cache_rows, slot_lengths, fresh_keys, offset):
    scores = (
        jnp.einsum("shc,stc->sht", query_rows, cache_rows, preferred_element_type=jnp.float32)
        * SCORE_SCALE
    )
    positions = offset + jnp.arange(cache_rows.shape[1], dtype=jnp.int32)
    live_mask = (positions[None, :] < slot_lengths[:, None])[:, None, :]
    masked = jnp.where(live_mask, scores, MASKED)
    block_peak = jnp.max(masked, axis=2)
    raw_weights = jnp.where(live_mask, jnp.exp(masked - block_peak[..., None]), 0.0)
    block_sum = jnp.sum(raw_weights, axis=2)
    block_values = jnp.einsum(
        "sht,stl->shl",
        raw_weights.astype(jnp.bfloat16),
        cache_rows[:, :, :LAT],
        preferred_element_type=jnp.float32,
    )
    merged_peak, merged_sum, merged_values = combined_all(
        (block_peak, block_sum, block_values), "ep", combine_partial
    )
    fresh_scores = (
        jnp.einsum("shc,sfc->shf", query_rows, fresh_keys, preferred_element_type=jnp.float32)
        * SCORE_SCALE
    )
    best_score = jnp.maximum(merged_peak, jnp.max(fresh_scores, axis=2))
    carried = jnp.exp(merged_peak - best_score)
    fresh_weight = jnp.exp(fresh_scores - best_score[..., None])
    fresh_values = fresh_keys[:, :, :LAT].astype(jnp.float32)
    numerator = carried[..., None] * merged_values + jnp.einsum(
        "shf,sfl->shl", fresh_weight, fresh_values, precision=lax.Precision.HIGHEST
    )
    denominator = carried * merged_sum + jnp.sum(fresh_weight, axis=2)
    return numerator / denominator[..., None]


def layer_local(
    attended,
    residual_rows,
    value_weight,
    output_weight,
    norm_gain,
    chosen,
    codes,
    gate_weight,
    up_weight,
    down_weight,
):
    heads_here = value_weight.shape[0]
    head_start = lax.axis_index("ep") * heads_here
    latent = lax.dynamic_slice_in_dim(attended, head_start, heads_here, 1).astype(jnp.bfloat16)
    values = jnp.einsum(
        "shl,hlv->shv", latent, value_weight, preferred_element_type=jnp.float32
    ).astype(jnp.bfloat16)
    columns = output_weight.shape[1]
    col_start = lax.axis_index("dp") * columns
    used_cols = lax.dynamic_slice_in_dim(
        lax.all_gather(values, "dp", axis=0, tiled=True), col_start, columns, 2
    )
    head_part = jnp.einsum(
        "shv,hvd->sd", used_cols, output_weight, preferred_element_type=jnp.float32
    )
    rank_count = lax.axis_size("dp")
    col_count = lax.axis_size("ep")
    total_rows = residual_rows.shape[0]
    width = residual_rows.shape[1]
    slot_count = total_rows // rank_count
    col_width = width // col_count
    row_first = lax.axis_index("dp") * slot_count
    col_first = lax.axis_index("ep") * col_width
    attn_sum = lax.psum(head_part, ("dp", "ep"))
    hidden = residual_rows.astype(jnp.float32) + attn_sum
    scale_rows = lax.rsqrt(jnp.mean(hidden * hidden, axis=1, keepdims=True) + NORM_EPS)
    normed = (hidden * scale_rows * norm_gain.astype(jnp.float32)).astype(jnp.bfloat16)
    own_hidden = lax.dynamic_slice(hidden, (row_first, col_first), (slot_count, col_width))
    code_wide = codes.astype(jnp.float32)
    shares = code_wide / jnp.sum(code_wide, axis=1, keepdims=True) * ROUTE_SCALE
    local_experts = gate_weight.shape[0]
    wanted = lax.axis_index("ep") * local_experts + jnp.arange(local_experts, dtype=jnp.int32)
    route_weight = jnp.sum(
        jnp.where(chosen[:, :, None] == wanted[None, None, :], shares[:, :, None], 0.0), axis=1
    )
    gate_proj = jnp.dot(normed, gate_weight[0], preferred_element_type=jnp.float32)
    up_proj = jnp.dot(normed, up_weight[0], preferred_element_type=jnp.float32)
    activated = (jax.nn.silu(gate_proj) * up_proj).astype(jnp.bfloat16)
    expert_out = jnp.dot(activated, down_weight[0], preferred_element_type=jnp.float32)
    expert_sum = route_weight * expert_out
    arranged = expert_sum.reshape(rank_count, slot_count, col_count, col_width)
    arranged = arranged.transpose(0, 2, 1, 3).reshape(
        rank_count * col_count * slot_count, col_width
    )
    routed = lax.psum_scatter(arranged, ("dp", "ep"), scatter_dimension=0, tiled=True)
    return (own_hidden + routed).astype(jnp.bfloat16)


def body(
    latent_cache,
    lengths,
    queries,
    fresh_latent,
    leaving,
    target,
    value_weight,
    output_weight,
    residual_stream,
    norm_gain,
    expert_ids,
    gate_codes,
    gate_weight,
    up_weight,
    down_weight,
):
    slot_count = latent_cache.shape[0]
    my_rank = lax.axis_index("dp")
    rank_count = lax.axis_size("dp")
    offset = lax.axis_index("ep") * latent_cache.shape[1]
    my_slots = my_rank * slot_count + jnp.arange(slot_count, dtype=jnp.int32)
    new_order = session_order(leaving, target, slot_count)
    out_slot = leaving[my_rank]
    lens_first = lengths[my_slots]
    attended_one = attend_local(
        queries[0], latent_cache, lens_first, fresh_latent[0][:, None, :], offset
    )
    outgoing = (
        lax.dynamic_slice_in_dim(latent_cache, out_slot, 1, 0),
        lax.dynamic_slice_in_dim(fresh_latent[0], out_slot, 1, 0),
    )
    moved_cache, moved_fresh = (
        lax.all_gather(outgoing[0], "dp", axis=0, tiled=True),
        lax.all_gather(outgoing[1], "dp", axis=0, tiled=True),
    )
    source = (
        jnp.zeros((rank_count,), jnp.int32).at[target].set(jnp.arange(rank_count, dtype=jnp.int32))
    )
    anchor = source[my_rank]
    cache_now = lax.dynamic_update_slice_in_dim(
        latent_cache, lax.dynamic_slice_in_dim(moved_cache, anchor, 1, 0), out_slot, 0
    )
    older_fresh = lax.dynamic_update_slice_in_dim(
        fresh_latent[0], lax.dynamic_slice_in_dim(moved_fresh, anchor, 1, 0), out_slot, 0
    )
    lens_second = lengths[new_order[my_slots]]
    queries_second = queries[1]
    newer_fresh = fresh_latent[1]
    fresh_second = jnp.stack([older_fresh, newer_fresh], axis=1)
    attended_two = attend_local(queries_second, cache_now, lens_second, fresh_second, offset)
    mixed_one = layer_local(
        attended_one,
        residual_stream[0],
        value_weight,
        output_weight,
        norm_gain,
        expert_ids[0],
        gate_codes[0],
        gate_weight,
        up_weight,
        down_weight,
    )
    mixed_two = layer_local(
        attended_two,
        residual_stream[1],
        value_weight,
        output_weight,
        norm_gain,
        expert_ids[1],
        gate_codes[1],
        gate_weight,
        up_weight,
        down_weight,
    )
    return jnp.stack([mixed_one, mixed_two])


def solution(mesh):
    placed = (
        P("dp", "ep", None),
        P(),
        P(None, "dp", None, None),
        P(None, "dp", None),
        P(),
        P(),
        P("ep", None, None),
        P("ep", "dp", None),
        P(),
        P(),
        P(),
        P(),
        P("ep", None, "dp"),
        P("ep", None, "dp"),
        P("ep", "dp", None),
    )
    return jax.shard_map(
        body, mesh=mesh, in_specs=placed, out_specs=P(None, "dp", "ep"), check_vma=False
    )
```

profile of v0, /device:TPU:1, one launch (start us, length us, event | category | flops | bytes accessed | tf_op | source)
XLA Modules:
  0.0 937.6 jit_solution(1346848704397500790)
XLA Ops:
  9.9 1.9 constant_dynamic-slice_fusion.8
  11.9 4.3 copy.50
  19.6 2.7 fusion.130
  22.3 1.6 fusion.8
  27.2 49.9 %all-gather.15.cloned.1.call-done = bf16[16,512,576]{1,2,0:T(8,128)(2,1)} async-done(((bf16[1,512,576]{1,2,0:T(8,128)(2,1)}), bf16[16,512,576]{1,2,0:T(8,128)(2,1)}) %all-gather.15.cloned.1.call-update) | async-done | bytes 9437200 | tf_op jit(solution)/shard_map/all_gather | solution.py:171
  77.0 1.9 constant_dynamic-slice_fusion.7
  81.2 3.1 fusion.128
  87.0 20.0 %all-gather.7 = f32[16,4,128]{2,1,0:T(4,128)S(1)} all-gather(f32[1,4,128]{2,1,0:T(4,128)S(1)} %bitcast.181), channel_id=2, replica_groups=mesh['dp'=16,'ep'=16] {'ep'}, dimensions={0}, use_global_device_ids=true | all-gather | bytes 34816 | tf_op jit(solution)/shard_map/all_gather | solution.py:16
  107.3 17.5 %all-gather.8 = f32[16,4,128]{2,1,0:T(4,128)S(1)} all-gather(f32[1,4,128]{2,1,0:T(4,128)S(1)} %bitcast.183), channel_id=3, replica_groups=mesh['dp'=16,'ep'=16] {'ep'}, dimensions={0}, use_global_device_ids=true | all-gather | bytes 34816 | tf_op jit(solution)/shard_map/all_gather | solution.py:16
  124.8 24.3 %all-gather.6 = bf16[16,1,576]{2,1,0:T(2,128)(2,1)S(1)} all-gather(bf16[1,1,576]{2,1,0:T(2,128)(2,1)S(1)} %constant_dynamic-slice_fusion.6), channel_id=8, replica_groups=mesh['dp'=16,'ep'=16] {'dp'}, dimensions={0}, use_global_device_ids=true | all-gather | bytes 19584 | tf_op jit(solution)/shard_map/all_gather | solution.py:172
  151.7 18.0 %all-gather.9 = f32[16,4,128]{2,1,0:T(4,128)S(1)} all-gather(f32[1,4,128]{2,1,0:T(4,128)S(1)} %bitcast.182), channel_id=5, replica_groups=mesh['dp'=16,'ep'=16] {'ep'}, dimensions={0}, use_global_device_ids=true | all-gather | bytes 34816 | tf_op jit(solution)/shard_map/all_gather | solution.py:16
  170.0 19.6 %all-gather.10 = f32[16,4,128]{2,1,0:T(4,128)S(1)} all-gather(f32[1,4,128]{2,1,0:T(4,128)S(1)} %bitcast.184), channel_id=6, replica_groups=mesh['dp'=16,'ep'=16] {'ep'}, dimensions={0}, use_global_device_ids=true | all-gather | bytes 34816 | tf_op jit(solution)/shard_map/all_gather | solution.py:16
  189.7 4.8 all-gather.17.cloned.1.call-done
  195.8 23.9 %while.38 = (s32[]{:T(128)}, f32[4,128]{1,0:T(4,128)S(1)}, f32[4,128]{1,0:T(4,128)S(1)}, f32[4,128,512]{2,1,0:T(8,128)S(1)}, f32[16,4,128]{2,1,0:T(4,128)S(1)}, ...) while((s32[]{:T(128)}, f32[4,128]{1,0:T(4,128)S(1)}, ...), condition=%wide.region_3.4_spmd, body=%wide.region_2.3_spmd.sunk | while | flops 789509 | bytes 3166359 | solution.py:22
  195.8 1.5 fusion.142
  197.4 1.5 fusion.142
  199.0 1.5 fusion.142
  200.6 1.5 fusion.142
  203.7 1.5 fusion.142
  205.3 1.5 fusion.142
  206.9 1.5 fusion.142
  208.4 1.6 fusion.142
  210.1 1.6 fusion.142
  211.8 1.5 fusion.142
  213.4 1.5 fusion.142
  214.9 1.5 fusion.142
  216.5 1.5 fusion.142
  218.1 1.5 fusion.142
  219.7 1.6 copy.52
  221.7 1.6 fusion.39
  223.3 18.3 %all_gather.54 = bf16[64,8,128]{2,1,0:T(8,128)(2,1)S(1)} all-gather(bf16[4,8,128]{2,1,0:T(8,128)(2,1)S(1)} %copy.55), channel_id=1, replica_groups=mesh['dp'=16,'ep'=16] {'dp'}, dimensions={0}, use_global_device_ids=true | all-gather | bytes 139264 | tf_op jit(solution)/shard_map/all_gather | solution.py:100
  241.7 3.4 convolution_bitcast_fusion.1
  245.2 67.8 %all-gather.19.cloned.1.call-done = f32[64,128,512]{2,1,0:T(8,128)} async-done(((f32[4,128,512]{2,1,0:T(8,128)}), f32[64,128,512]{2,1,0:T(8,128)}) %all-gather.19.cloned.1.call-update) | async-done | bytes 16777232 | tf_op jit(solution)/shard_map/all_gather | solution.py:16
  314.3 23.7 %while.39 = (s32[]{:T(128)}, f32[4,128]{1,0:T(4,128)S(1)}, f32[4,128]{1,0:T(4,128)S(1)}, f32[4,128,512]{2,1,0:T(8,128)S(1)}, f32[16,4,128]{2,1,0:T(4,128)S(1)}, ...) while((s32[]{:T(128)}, f32[4,128]{1,0:T(4,128)S(1)}, ...), condition=%wide.region_14.15_spmd, body=%wide.region_13.14_spmd.sunk | while | flops 789509 | bytes 3166359 | solution.py:22
  340.4 18.3 %all_gather.63 = bf16[64,8,128]{2,1,0:T(8,128)(2,1)S(1)} all-gather(bf16[4,8,128]{2,1,0:T(8,128)(2,1)S(1)} %copy.65), channel_id=1, replica_groups=mesh['dp'=16,'ep'=16] {'dp'}, dimensions={0}, use_global_device_ids=true | all-gather | bytes 139264 | tf_op jit(solution)/shard_map/all_gather | solution.py:100
  358.8 2.0 convolution_bitcast_fusion
  361.6 261.1 %all-reduce.9.cloned.1.call-done = (f32[64,7168]{1,0:T(8,128)}, f32[64,7168]{1,0:T(8,128)}) async-done(((f32[64,7168]{1,0:T(8,128)}, f32[64,7168]{1,0:T(8,128)}), (f32[64,7168]{1,0:T(8,128)}, f32[64,7168]{1,0:T(8,128)})) %all-reduce.9.cloned.1.call-update) | async-done | bytes 3670032 | tf_op jit(solution)/shard_map/psum | solution.py:113
  622.7 4.7 multiply_reduce_fusion.1
  628.6 4.1 convolution_multiply_fusion
  632.7 3.2 reshape.273
  636.0 4.3 copy.85
  640.3 3.0 reshape.274
  643.3 2.5 fusion.18
  645.8 4.2 convolution_multiply_fusion.1
  650.0 3.2 reshape.271
  653.2 4.3 copy.86
  657.5 3.0 reshape.272
  660.5 268.3 %all-reduce.7.cloned.1.call-done = (f32[1024,448]{1,0:T(8,128)}, f32[1024,448]{1,0:T(8,128)}) async-done(((f32[1024,448]{1,0:T(8,128)}, f32[1024,448]{1,0:T(8,128)}), (f32[1024,448]{1,0:T(8,128)}, f32[1024,448]{1,0:T(8,128)})) %all-reduce.7.cloned.1.call-update) | async-done | bytes 3670032
  (152 shorter events, 49.1 us)
Async XLA Ops:
  6.5 622.1 %copy-start = (bf16[1,128,7168]{2,1,0:T(8,128)(2,1)S(1)}, bf16[1,128,7168]{2,1,0:T(8,128)(2,1)}, u32[]{:S(2)}) copy-start(bf16[1,128,7168]{2,1,0:T(8,128)(2,1)} %param.33) | copy-start | bytes 5505028
  6.5 70.5 %all-gather.15.cloned.1.call-start = ((), (), s32[]{:S(2)}) async-start(), calls=%async_computation | async-start | bytes 10027008 | tf_op jit(solution)/shard_map/all_gather | solution.py:171
  11.8 182.7 %all-gather.17.cloned.1.call-start = ((), (), s32[]{:S(2)}) async-start(), calls=%async_computation.1 | async-start | bytes 17825792 | tf_op jit(solution)/shard_map/all_gather | solution.py:16
  11.9 4.4 copy-start.13
  11.9 4.4 copy-start.2
  11.9 5.1 copy-start.1
  19.6 2.7 copy-start.3
  23.9 289.1 %all-gather.19.cloned.1.call-start = ((), (), s32[]{:S(2)}) async-start(), calls=%async_computation.2 | async-start | bytes 17825792 | tf_op jit(solution)/shard_map/all_gather | solution.py:16
  81.2 4.1 copy-start.4
  84.3 1.0 copy-start.7
  85.3 1.6 copy-start.11
  86.8 535.9 %all-reduce.9.cloned.1.call-start = ((), (), s32[]{:S(2)}) async-start(), calls=%async_computation.4 | async-start | bytes 7340032 | tf_op jit(solution)/shard_map/psum | solution.py:113
  87.0 82.7 %copy-start.8 = (f32[4,128,512]{2,1,0:T(8,128)S(1)}, f32[4,128,512]{2,1,0:T(8,128)}, u32[]{:S(2)}) copy-start(f32[4,128,512]{2,1,0:T(8,128)} %copy-done.7) | copy-start | bytes 3145732
  338.0 20.9 %copy-start.14 = (bf16[8,8,7168]{2,1,0:T(8,128)(2,1)S(1)}, bf16[8,8,7168]{2,1,0:T(8,128)(2,1)}, u32[]{:S(2)}) copy-start(bf16[8,8,7168]{2,1,0:T(8,128)(2,1)} %param.26) | copy-start | bytes 2752516
  360.8 0.7 copy-start.10
  360.8 0.7 copy-start.9
  360.8 0.7 copy-start.12
  360.9 567.9 %all-reduce.7.cloned.1.call-start = ((), (), s32[]{:S(2)}) async-start(), calls=%async_computation.3 | async-start | bytes 8388608
  622.7 4.7 copy-start.6
  627.4 1.2 copy-start.5
Sparse Core Ops, SparseCore 0:
  11.9 65.0 all-gather.14
  79.5 114.9 all-gather.16
  196.9 116.0 all-gather.18
  361.0 261.6 all-reduce.8
  660.6 268.1 all-reduce.6
where the time goes:
time: 941 us; the launch traced here: 938 us
  waiting for transfers between devices  652 us (69%)
  blocking collectives  136 us (14%)
  other arithmetic  54.6 us (6%)
  local copies, waits for them, and re-layouts  44.5 us (5%)
  matrix products  31.9 us (3%)
  between operations  17.4 us (2%)
    unnamed x6, waiting for transfers between devices  268 us
    psum x1, waiting for transfers between devices, layer_local(): attn_sum = lax.psum(head_part, ('dp', 'ep'))  261 us
    all_gather x4, blocking collectives, combined_all(): everything = jax.tree.map(lambda part: lax.all_gather(part, axis), value)  75.1 us
    all_gather x2, waiting for transfers between devices, combined_all(): everything = jax.tree.map(lambda part: lax.all_gather(part, axis), value)  72.7 us
    all_gather x1, waiting for transfers between devices, body(): lax.all_gather(outgoing[0], 'dp', axis=0, tiled=True)  49.9 us
    add x30, other arithmetic, combine_partial(): scale_early[..., None] * values_early + scale_late[..., None] * values_late  45.9 us
    all_gather x2, blocking collectives, layer_local(): lax.all_gather(values, 'dp', axis=0, tiled=True)  36.6 us
    all_gather x1, blocking collectives, body(): lax.all_gather(outgoing[1], 'dp', axis=0, tiled=True)  24.3 us
  transfers between devices with their start and end apart: 5, of which 5 were waited for; matrix products, arithmetic and copies ran while one was open for 6% of the time, Pallas kernels for 0%

commit v1 on v0

v1 whole, which is shorter than its diff:
```python
import functools

import jax
import jax.numpy as jnp
from jax import lax
from jax.experimental import pallas as pl
from jax.experimental.pallas import tpu as pltpu
from jax.sharding import PartitionSpec as P

MESH = pl.DeviceIdType.MESH
SCORE_SCALE = 192.0 ** (-0.5)
ROUTE_SCALE = 2.5
NORM_EPS = 1e-06
MASKED = -1e30
LAT = 512
BF = jnp.bfloat16
F32 = jnp.float32


def iota(shape, dim):
    return lax.broadcasted_iota(jnp.int32, shape, dim)


def dot(a, b, ca=1, cb=0):
    return lax.dot_general(a, b, (((ca,), (cb,)), ((), ())), preferred_element_type=F32)


def loop(lo, hi, fn):
    lax.fori_loop(lo, hi, lambda i, c: (fn(i), c)[1], 0)


def kernel(
    DP, EP,
    lengths, leaving, target, fresh, ids, codes, gain, resid,
    cache_h, q_h, vw_h, ow_h, gate_h, up_h, down_h,
    out,
    q1v, q2v, cv, vw, ow, gu, dn,
    a1s, a1r, a2s, a2r, fk,
    bs, bt, br, btr, sc, lat,
    cs, cr,
    pc, pr, xs, xr, zs, zr,
    pc2, pr2, xs2, xr2, zs2, zr2,
    gs, gr, hb, rw,
    ld, sa1, ra1, sa2, ra2, sb, rb, st, rt, scs, rcs,
    s1c, r1c, s1x, r1x, s1z, r1z,
    s2c, r2c, s2x, r2x, s2z, r2z,
    sgz, rgz, sgx, rgx, sgc, rgc,
):
    NZ = DP // 2
    SL = 4
    HP = vw.shape[0]
    VD = vw.shape[2]
    VC = VD // DP
    ROWS = DP * 8
    HALF = ROWS // 2
    BW = gain.shape[1]
    LW = cv.shape[1]
    T = cv.shape[2]
    HEADS = q1v.shape[2]
    PIECE = a2s.shape[0]
    dp = lax.axis_index("dp")
    ep = lax.axis_index("ep")
    z = dp // 2
    core = dp % 2

    def to_dp(k):
        return (dp + k) % DP

    def to_ep(k):
        return (ep + k) % EP

    def remote(src, dst, s, r, d, e):
        return pltpu.make_async_remote_copy(
            src_ref=src, dst_ref=dst, send_sem=s, recv_sem=r, device_id=(d, e), device_id_type=MESH
        )

    def local(src, dst, k):
        return pltpu.make_async_copy(src, dst, ld.at[k])

    loads = [local(q_h.at[1], q2v, 0), local(q_h.at[0], q1v, 1)]
    loads += [local(cache_h.at[s], cv.at[s], 2 + s) for s in range(SL)]
    loads += [
        local(vw_h, vw, 6),
        local(ow_h, ow, 7),
        local(gate_h, gu.at[:, pl.ds(0, 128)], 8),
        local(up_h, gu.at[:, pl.ds(128, 128)], 9),
        local(down_h, dn, 10),
    ]
    for c in loads:
        c.start()

    barrier = pltpu.get_barrier_semaphore()
    loop(1, DP, lambda k: pl.semaphore_signal(barrier, inc=1, device_id=(to_dp(k), ep), device_id_type=MESH))
    loop(1, EP, lambda k: pl.semaphore_signal(barrier, inc=1, device_id=(dp, to_ep(k)), device_id_type=MESH))

    lv = leaving[dp]
    f0 = fresh[0].astype(F32)
    f1 = fresh[1].astype(F32)
    frow = jnp.sum(jnp.where(iota(f1.shape, 0) == lv, f1, 0.0), axis=0, keepdims=True)
    frow = jnp.concatenate([frow, jnp.zeros((1, 640 - LW), F32)], axis=1)
    fpieces = [frow[:, 128 * i : 128 * (i + 1)] for i in range(5)]
    loads[0].wait()
    a1s[0:LW, 0:HEADS] = q2v[lv]
    a1s[LW : LW + 16] = jnp.concatenate(fpieces + [jnp.zeros((11, 128), F32)], axis=0).astype(BF)
    a1s[LW + 16 :] = jnp.zeros((a1s.shape[0] - LW - 16, 128), BF)
    mine = pl.ds(pl.multiple_of(ep * PIECE, 16), PIECE)
    a1r[dp] = a1s[mine]
    pl.semaphore_wait(barrier, DP + EP - 2)

    def a1(k):
        d = to_dp(k)
        return remote(a1s.at[mine], a1r.at[dp], sa1.at[d], ra1.at[dp], d, ep)

    loop(1, DP, lambda k: a1(k).start())

    def attend(q, s, live_fresh):
        kt = cv[s]
        score = dot(q, kt, 0, 0) * SCORE_SCALE
        pos = ep * T + iota(score.shape, 1)
        live = pos < lengths[dp * SL + s]
        fkeys = fk[...]
        fscore = dot(q, fkeys, 0, 1) * SCORE_SCALE
        score = jnp.where(live, score, MASKED)
        fscore = jnp.where(live_fresh, fscore, MASKED)
        peak = jnp.maximum(
            jnp.max(score, axis=1, keepdims=True), jnp.max(fscore, axis=1, keepdims=True)
        )
        w = jnp.where(live, jnp.exp(score - peak), 0.0)
        fw = jnp.where(live_fresh, jnp.exp(fscore - peak), 0.0)
        total = jnp.sum(w, axis=1, keepdims=True) + jnp.sum(fw, axis=1, keepdims=True)
        v = dot(w.astype(BF), kt[:LAT], 1, 1) + dot(fw.astype(BF), fkeys[:, :LAT])
        return peak, total, v

    group = iota((HEADS, 128), 1) >> 4

    def attend_step(k, query_of, live_of):
        stat = jnp.zeros((HEADS, 128), F32)
        for p in range(SL // 2):
            both = []
            for s in (2 * p, 2 * p + 1):
                peak, total, v = attend(query_of(s), s, live_of(s))
                stat = jnp.where(group == 2 * s, peak, jnp.where(group == 2 * s + 1, total, stat))
                both.append(v.reshape(EP, HP, LAT))
            bs[k, :, 16 * p : 16 * p + 16, :] = jnp.concatenate(both, axis=1).astype(BF)
        bt[k] = stat.reshape(EP, HP, 128)
        br[k, ep] = bs[k, ep]
        btr[k, ep] = bt[k, ep]

    def b_copy(k, i):
        e = to_ep(i)
        return remote(bs.at[k, e], br.at[k, ep], sb.at[k, e], rb.at[k, ep], dp, e)

    def t_copy(k, i):
        e = to_ep(i)
        return remote(bt.at[k, e], btr.at[k, ep], st.at[k, e], rt.at[k, ep], dp, e)

    def b_wait(k, i):
        e = to_ep(i)
        remote(bs.at[k, e], br.at[k, e], sb.at[k, e], rb.at[k, e], dp, e).wait_recv()
        remote(bt.at[k, e], btr.at[k, e], st.at[k, e], rt.at[k, e], dp, e).wait_recv()

    def b_start(k):
        def go(i):
            t_copy(k, i).start()
            b_copy(k, i).start()

        loop(1, EP, go)

    fcol = iota((1, 16), 1)
    at_zero = ep == 0
    fk[...] = jnp.concatenate([f0, f1, jnp.zeros((8, LW), F32)], axis=0).astype(BF)
    loads[1].wait()
    for s in range(SL):
        loads[2 + s].wait()
    attend_step(0, lambda s: q1v[s], lambda s: (fcol == s) & at_zero)

    def a1_wait(k):
        d = to_dp(k)
        remote(a1s.at[mine], a1r.at[d], sa1.at[d], ra1.at[d], d, ep).wait_recv()

    loop(1, DP, a1_wait)
    piece = a1r[target[dp]]
    a2s[...] = piece
    a2r[mine] = piece

    def a2(k):
        e = to_ep(k)
        return remote(a2s, a2r.at[mine], sa2.at[e], ra2.at[ep], dp, e)

    def a2_wait(k):
        e = to_ep(k)
        rows = pl.ds(pl.multiple_of(e * PIECE, 16), PIECE)
        remote(a2s, a2r.at[rows], sa2.at[e], ra2.at[e], dp, e).wait_recv()

    loop(1, EP, lambda k: a2(k).start())
    b_start(0)

    row = iota((ROWS, 2 * SL * DP), 0)
    col = iota((ROWS, 2 * SL * DP), 1)
    half_bits = HALF.bit_length() - 1
    r_core = row >> half_bits
    r_z = (row >> 3) & (NZ - 1)
    r_step = (row >> 2) & 1
    slot = (r_z * 2 + r_core) * SL + (row & 3)
    held = slot
    for r in range(DP):
        t = target[r]
        held = jnp.where(slot == t * SL + leaving[t], r * SL + leaving[r], held)
    place = (r_step * (SL * DP) + jnp.where(r_step == 1, held, slot)) == col
    code = codes[...].astype(F32)
    share = code / jnp.sum(code, axis=1, keepdims=True) * ROUTE_SCALE
    weight = jnp.sum(jnp.where(ids[...] == ep, share, 0.0), axis=1)
    weight = jnp.concatenate([weight[0:1], weight[1:2]], axis=1)
    own_place = (r_step * (SL * DP) + slot) == col
    rw[...] = jnp.broadcast_to(
        jnp.sum(jnp.where(own_place, weight, 0.0), axis=1, keepdims=True), (ROWS, 128)
    )
    place = jnp.where(place, 1.0, 0.0).astype(BF)

    loop(1, EP, a2_wait)
    moved_f = a2r[LW : LW + 16].astype(F32)
    moved_f = jnp.concatenate([moved_f[i : i + 1] for i in range(5)], axis=1)[:, :LW]
    fk[...] = jnp.concatenate([f0, f1, moved_f, jnp.zeros((7, LW), F32)], axis=0).astype(BF)
    moved_q = a2r[0:LW, 0:HEADS]
    attend_step(
        1,
        lambda s: jnp.where(lv == s, moved_q, q2v[s]),
        lambda s: ((fcol == s) | (fcol == jnp.where(lv == s, 8, 4 + s))) & at_zero,
    )
    b_start(1)

    head_of = iota((SL * HP, VD), 0) & (HP - 1)

    def c_copy(k, i):
        d = to_dp(i)
        return remote(cs.at[k], cr.at[k, dp], scs.at[k, d], rcs.at[k, dp], d, ep)

    def c_wait(k, i):
        d = to_dp(i)
        remote(cs.at[k], cr.at[k, d], scs.at[k, d], rcs.at[k, d], d, ep).wait_recv()

    def merge(k):
        loop(1, EP, lambda i: b_wait(k, i))
        stats = btr[k]
        w = jnp.exp(stats - jnp.max(stats, axis=0, keepdims=True))
        shifted = jnp.concatenate([stats[:, :, 16:], stats[:, :, :16]], axis=2)
        sc[...] = w / jnp.sum(w * shifted, axis=0, keepdims=True)

        def add(j, acc):
            one = sc[j]
            scale = jnp.concatenate([one[:, 32 * s : 32 * s + 1] for s in range(SL)], axis=0)
            return acc + scale * br[k, j].astype(F32)

        latent = lax.fori_loop(0, EP, add, jnp.zeros((SL * HP, LAT), F32)).astype(BF)
        values = jnp.zeros((SL * HP, VD), F32)
        for h in range(HP):
            values = jnp.where(head_of == h, dot(latent, vw[h]), values)
        values = values.astype(BF)
        cs[k] = values
        cr[k, dp] = values
        loop(1, DP, lambda i: c_copy(k, i).start())

    loads[6].wait()
    merge(0)
    merge(1)
    loads[7].wait()

    lanes = HP * VC
    pick = jnp.where(
        iota((VD, lanes), 0) == dp * VC + (iota((VD, lanes), 1) & (VC - 1)), 1.0, 0.0
    ).astype(BF)
    vc_bits = VC.bit_length() - 1
    keep = (iota((DP * SL * HP, lanes), 0) & (HP - 1)) == (iota((DP * SL * HP, lanes), 1) >> vc_bits)
    used = []
    for k in range(2):
        loop(1, DP, lambda i: c_wait(k, i))
        picked = dot(cr[k].reshape(DP * SL * HP, VD), pick)
        picked = jnp.where(keep, picked, 0.0)
        used.append(jnp.sum(picked.reshape(DP * SL, HP, lanes), axis=1))
    used = dot(place, jnp.concatenate(used, axis=0).astype(BF)).astype(BF)

    own_rows = pl.ds(pl.multiple_of(core * HALF, 16), HALF)
    other_rows = pl.ds(pl.multiple_of((1 - core) * HALF, 16), HALF)
    sibling = z * 2 + (1 - core)

    def reduce_scatter(product, pc, pr, xs, xr, zs, zr, s_c, r_c, s_x, r_x, s_z, r_z):
        def c_copy(j):
            return remote(pc.at[j, other_rows], pr.at[j], s_c.at[j], r_c.at[j], sibling, ep)

        def x_copy(j):
            return remote(xs.at[j], xr.at[ep], s_x.at[j], r_x.at[ep], dp, j)

        def z_copy(i):
            t = (z + i) % NZ
            return remote(zs.at[t], zr.at[z], s_z.at[t], r_z.at[z], t * 2 + core, ep)

        def pair(i):
            return (ep // 2 + 1 + i) % (EP // 2)

        def first(i):
            jp = pair(i)
            part = product(pl.ds(pl.multiple_of(jp * 2 * BW, 128), 2 * BW))
            pc[2 * jp] = part[:, :BW].astype(BF)
            pc[2 * jp + 1] = part[:, BW:].astype(BF)
            c_copy(2 * jp).start()
            c_copy(2 * jp + 1).start()

        loop(0, EP // 2, first)

        def second(i):
            for t in range(2):
                j = 2 * pair(i) + t
                c_copy(j).wait_recv()
                part = (pc[j, own_rows].astype(F32) + pr[j].astype(F32)).astype(BF)
                xs[j] = part

                @pl.when(j != ep)
                def _():
                    x_copy(j).start()

        loop(0, EP // 2, second)
        xr[ep] = xs[ep]

        def x_wait(i):
            j = to_ep(i)
            remote(xs.at[j], xr.at[j], s_x.at[j], r_x.at[j], dp, j).wait_recv()

        loop(1, EP, x_wait)
        total = lax.fori_loop(
            0, EP, lambda j, acc: acc + xr[j].astype(F32), jnp.zeros((HALF, BW), F32)
        )
        zs[...] = total.reshape(NZ, 8, BW)
        zr[z] = zs[z]
        loop(1, NZ, lambda i: z_copy(i).start())

        def z_wait(i):
            t = (z + i) % NZ
            remote(zs.at[t], zr.at[t], s_z.at[t], r_z.at[t], t * 2 + core, ep).wait_recv()

        loop(1, NZ, z_wait)
        result = jnp.sum(zr[...], axis=0)

        def finish():
            loop(0, EP, lambda j: c_copy(j).wait_send())
            loop(1, EP, lambda i: x_copy(to_ep(i)).wait_send())
            loop(1, NZ, lambda i: z_copy(i).wait_send())

        return result, finish

    attn, finish_one = reduce_scatter(
        lambda cols: dot(used, ow[:, cols]),
        pc, pr, xs, xr, zs, zr, s1c, r1c, s1x, r1x, s1z, r1z,
    )
    own_resid = jnp.concatenate([resid[0].astype(F32), resid[1].astype(F32)], axis=0)
    hidden = own_resid + attn

    gs[:, :BW] = hidden * gain[...]
    gs[:, BW:] = jnp.broadcast_to(
        jnp.sum(hidden * hidden, axis=1, keepdims=True), (8, gs.shape[1] - BW)
    )
    gr[z] = gs[...]

    def gz_copy(i):
        t = (z + i) % NZ
        return remote(gs, gr.at[z], sgz.at[t], rgz.at[z], t * 2 + core, ep)

    def gz_wait(i):
        t = (z + i) % NZ
        remote(gs, gr.at[t], sgz.at[t], rgz.at[t], t * 2 + core, ep).wait_recv()

    def gx_copy(i):
        e = to_ep(i)
        block = hb.at[ep, own_rows]
        return remote(block, block, sgx.at[e], rgx.at[ep], dp, e)

    def gx_wait(e):
        block = hb.at[e, own_rows]
        remote(block, block, sgx.at[e], rgx.at[e], dp, e).wait_recv()

    def gc_copy(e):
        block = hb.at[e, own_rows]
        return remote(block, block, sgc.at[e], rgc.at[e], sibling, ep)

    def gc_wait(e):
        block = hb.at[e, other_rows]
        remote(block, block, sgc.at[e], rgc.at[e], sibling, ep).wait_recv()

    loop(1, NZ, lambda i: gz_copy(i).start())
    loop(1, NZ, gz_wait)
    wide = gr[...].reshape(HALF, gs.shape[1])
    hi = wide.astype(BF).astype(F32)
    mid = (wide - hi).astype(BF).astype(F32)
    lo = wide - hi - mid
    lane = iota(wide.shape, 1)
    hb[ep, own_rows] = jnp.where(
        lane <= BW, hi, jnp.where(lane == BW + 1, mid, lo)
    ).astype(BF)
    loop(1, EP, lambda i: gx_copy(i).start())
    gc_copy(ep).start()
    loads[8].wait()
    loads[9].wait()

    def project(e, acc):
        proj, squares = acc
        block = hb[e]
        w = gu[pl.ds(pl.multiple_of(e * BW, 16), BW), :]
        tail = block[:, 384:].astype(F32)
        return proj + dot(block[:, :BW], w), squares + tail

    def step(i, acc):
        e = (ep + EP - i) % EP
        gx_wait(e)
        gc_copy(e).start()
        before = (ep + EP - i + 1) % EP
        gc_wait(before)
        return project(before, acc)

    acc = (jnp.zeros((ROWS, 256), F32), jnp.zeros((ROWS, 128), F32))
    acc = lax.fori_loop(1, EP, step, acc)
    last = (ep + 1) % EP
    gc_wait(last)
    proj, squares = project(last, acc)
    off = BW - 384
    square = squares[:, off : off + 1] + squares[:, off + 1 : off + 2] + squares[:, off + 2 : off + 3]
    scale = lax.rsqrt(square / float(BW * EP) + NORM_EPS)
    g = proj[:, :128] * scale
    u = proj[:, 128:] * scale
    act = (g / (1.0 + jnp.exp(-g)) * u).astype(BF)
    loads[10].wait()
    route = rw[:, 0:1]
    routed, finish_two = reduce_scatter(
        lambda cols: dot(act, dn[:, cols]) * route,
        pc2, pr2, xs2, xr2, zs2, zr2, s2c, r2c, s2x, r2x, s2z, r2z,
    )
    mixed = (hidden + routed).astype(out.dtype)
    out[0] = mixed[0:4]
    out[1] = mixed[4:8]

    loop(1, DP, lambda k: a1(k).wait_send())
    loop(1, EP, lambda k: a2(k).wait_send())
    for k in range(2):
        loop(1, EP, lambda i: b_copy(k, i).wait_send())
        loop(1, EP, lambda i: t_copy(k, i).wait_send())
        loop(1, DP, lambda i: c_copy(k, i).wait_send())
    finish_one()
    loop(1, NZ, lambda i: gz_copy(i).wait_send())
    loop(1, EP, lambda i: gx_copy(i).wait_send())
    loop(0, EP, lambda e: gc_copy(e).wait_send())
    finish_two()


def body(
    DP, EP,
    latent_cache, lengths, queries, fresh_latent, leaving, target, value_weight, output_weight,
    residual_stream, norm_gain, expert_ids, gate_codes, gate_weight, up_weight, down_weight,
):
    SL, T, LW = latent_cache.shape
    H = queries.shape[2]
    HP, _, VD = value_weight.shape
    D = norm_gain.shape[0]
    BW = D // EP
    NZ = DP // 2
    ROWS = DP * 8
    HALF = ROWS // 2
    PIECE = 768 // EP
    dp = lax.axis_index("dp")
    ep = lax.axis_index("ep")
    cache = jnp.swapaxes(latent_cache, 1, 2)
    q = jnp.swapaxes(queries, 2, 3)
    gain = lax.dynamic_slice_in_dim(norm_gain, ep * BW, BW, 0).astype(F32).reshape(1, BW)
    resid = lax.dynamic_slice(residual_stream, (0, dp * SL, ep * BW), (2, SL, BW))
    ow = output_weight.reshape(HP * output_weight.shape[1], D)
    smem = pl.BlockSpec(memory_space=pltpu.SMEM)
    vmem = pl.BlockSpec(memory_space=pltpu.VMEM)
    anyw = pl.BlockSpec(memory_space=pl.ANY)
    V = pltpu.VMEM
    sems = lambda *n: pltpu.SemaphoreType.DMA(n)
    rs_bufs = [
        V((EP, ROWS, BW), BF), V((EP, HALF, BW), BF), V((EP, HALF, BW), BF), V((EP, HALF, BW), BF),
        V((NZ, 8, BW), F32), V((NZ, 8, BW), F32),
    ]
    rs_sems = [sems(EP), sems(EP), sems(EP), sems(EP), sems(NZ), sems(NZ)]
    scratch = [
        V((SL, LW, H), BF), V((SL, LW, H), BF), V((SL, LW, T), BF), V(value_weight.shape, BF), V(ow.shape, BF),
        V((D, 256), BF), V((128, D), BF),
        V((768, 128), BF), V((DP, PIECE, 128), BF), V((PIECE, 128), BF), V((768, 128), BF), V((16, LW), BF),
        V((2, EP, SL * HP, LAT), BF), V((2, EP, HP, 128), F32), V((2, EP, SL * HP, LAT), BF),
        V((2, EP, HP, 128), F32), V((EP, HP, 128), F32), V((SL * HP, LAT), BF),
        V((2, SL * HP, VD), BF), V((2, DP, SL * HP, VD), BF),
        *rs_bufs, *rs_bufs,
        V((8, 512), F32), V((NZ, 8, 512), F32), V((EP, ROWS, 512), BF), V((ROWS, 128), F32),
        sems(11), sems(DP), sems(DP), sems(EP), sems(EP), sems(2, EP), sems(2, EP), sems(2, EP), sems(2, EP),
        sems(2, DP), sems(2, DP),
        *rs_sems, *rs_sems,
        sems(NZ), sems(NZ), sems(EP), sems(EP), sems(EP), sems(EP),
    ]
    return pl.pallas_call(
        functools.partial(kernel, DP, EP),
        out_shape=jax.ShapeDtypeStruct((2, SL, BW), BF),
        in_specs=[smem] * 3 + [vmem] * 5 + [anyw] * 7,
        out_specs=vmem,
        scratch_shapes=scratch,
        compiler_params=pltpu.CompilerParams(
            collective_id=0, has_side_effects=True, vmem_limit_bytes=56 * 2**20
        ),
        name="decode",
    )(
        lengths, leaving, target, fresh_latent,
        jnp.swapaxes(expert_ids, 1, 2), jnp.swapaxes(gate_codes, 1, 2), gain, resid,
        cache, q, value_weight, ow, gate_weight[0], up_weight[0], down_weight[0],
    )


def solution(mesh):
    placed = (
        P("dp", "ep", None), P(), P(None, "dp", None, None), P(None, "dp", None), P(), P(),
        P("ep", None, None), P("ep", "dp", None), P(), P(), P(), P(),
        P("ep", None, "dp"), P("ep", None, "dp"), P("ep", "dp", None),
    )
    return jax.shard_map(
        functools.partial(body, mesh.shape["dp"], mesh.shape["ep"]),
        mesh=mesh, in_specs=placed, out_specs=P(None, "dp", "ep"), check_vma=False,
    )
```

time: 941 us -> 126 us (0.13)
  waiting for transfers between devices: 652 us -> 0 us
  blocking collectives: 136 us -> 0 us
  Pallas kernels: 0 us -> 123 us
  other arithmetic: 54.6 us -> 1.45 us
  local copies, waits for them, and re-layouts: 44.5 us -> 2.04 us
  matrix products: 31.9 us -> 0 us
  between operations: 17.4 us -> 0.01 us
    unnamed x6 -> x0, waiting for transfers between devices: 268 us -> none
    psum x1 -> x0, waiting for transfers between devices: 261 us -> none  [layer_local(): attn_sum = lax.psum(head_part, ('dp', 'ep'))]
    all_gather x7 -> x0, blocking collectives: 136 us -> none  [the longest x4 75.1 us: combined_all(): everything = jax.tree.map(lambda part: lax.all_gather(part, axis), value)]
    pallas_call x0 -> x1, Pallas kernels: none -> 123 us  [body(): pl.pallas_call(functools.partial(kernel, DP, EP), out_shape=jax.ShapeDtyp...]
    all_gather x3 -> x0, waiting for transfers between devices: 123 us -> none  [the longest x2 72.7 us: combined_all(): everything = jax.tree.map(lambda part: lax.all_gather(part, axis), value)]
    add x63 -> x0, other arithmetic: 46.7 us -> none  [the longest x30 45.9 us: combine_partial(): scale_early[..., None] * values_early + scale_late[..., None] * values_late]
    dot_general x15 -> x0, matrix products: 31.9 us -> none  [the longest x2 8.31 us: layer_local(): jnp.dot(activated, down_weight[0], preferred_element_type=jnp.float32)]
    reshape x7 -> x0, local copies, waits for them, and re-layouts: 21 us -> none  [the longest x4 15 us: layer_local(): arranged = expert_sum.reshape(rank_count, slot_count, col_count, col_width)]
  transfers between devices with their start and end apart: 5 -> 0, of which waited for: 5 -> 0; matrix products, arithmetic and copies ran while one was open for 6% -> 0% of each run, Pallas kernels for 0% -> 0%
where the time goes in v1:
time: 126 us
  Pallas kernels  123 us (98%)
  local copies, waits for them, and re-layouts  2.04 us (2%)
  other arithmetic  1.45 us (1%)
    pallas_call x1, Pallas kernels, body(): pl.pallas_call(functools.partial(kernel, DP, EP), out_shape=jax.ShapeDtyp...  123 us

profile of v1, /device:TPU:1, one launch (start us, length us, event | category | flops | bytes accessed | tf_op | source)
XLA Modules:
  0.0 126.1 jit_solution(10145922394974912668)
XLA Ops:
  0.0 0.0 copy-start
  0.0 1.5 %dynamic-slice_convert_fusion = f32[448]{0:T(512)} fusion(bf16[7168]{0:T(1024)(128)(2,1)} %param.24, s32[]{:T(128)S(6)} %select_n.7), kind=kLoop, calls=%fused_computation | loop fusion | flops 448 | bytes 2692 | tf_op jit(solution)/shard_map/reshape | solution.py:470
  1.5 0.1 copy-done
  1.5 0.7 constant_dynamic-slice_fusion.resid
  2.2 122.6 %decode.1 = bf16[2,4,448]{2,1,0:T(4,128)(2,1)} custom-call(s32[64]{0:T(128)} %lengths.1, s32[16]{0:T(128)} %leaving.1, s32[16]{0:T(128)} %target.1, bf16[2,4,576]{2,1,0:T(4,128)(2,1)} %fresh.1, s32[2,8,64]{2,1,0:T(8,128)} %bitcast.15, s32[2,8,64]{2,1,0:T(8,128)} %bitcast.16, f32[1,448]{1,0:T(1,128)} %bitcast.17, ...), custom_call_target="tpu_custom_call" | custom-call | tf_op jit(solution)/shard_map/decode/pallas_call | solution.py:497
  124.8 1.3 %copy.17 = bf16[2,4,448]{2,1,0:T(4,128)(2,1)} copy(bf16[2,4,448]{2,1,0:T(4,128)(2,1)} %decode.1) | data formatting | bytes 14336
Async XLA Ops:
  0.0 1.5 %copy-start = (bf16[2,64,7168]{2,1,0:T(8,128)(2,1)S(1)}, bf16[2,64,7168]{2,1,0:T(8,128)(2,1)}, u32[]{:S(2)}) copy-start(bf16[2,64,7168]{2,1,0:T(8,128)(2,1)} %param.23) | copy-start | bytes 5505028

commit v2 on v1

--- a/solution.py
+++ b/solution.py
@@ -34,16 +34,16 @@
     lengths, leaving, target, fresh, ids, codes, gain, resid,
     cache_h, q_h, vw_h, ow_h, gate_h, up_h, down_h,
     out,
-    q1v, q2v, cv, vw, ow, gu, dn,
+    q1v, q2v, cv, vw, gu, rv,
+    owr, dnr, us, ur, az, ar,
     a1s, a1r, a2s, a2r, fk,
     bs, bt, br, btr, sc, lat,
     cs, cr,
-    pc, pr, xs, xr, zs, zr,
-    pc2, pr2, xs2, xr2, zs2, zr2,
+    es1, er1, es2, er2,
     gs, gr, hb, rw,
     ld, sa1, ra1, sa2, ra2, sb, rb, st, rt, scs, rcs,
-    s1c, r1c, s1x, r1x, s1z, r1z,
-    s2c, r2c, s2x, r2x, s2z, r2z,
+    sow, row_, sdn, rdn, su, ru, sact, ract,
+    s1, r1, s2, r2,
     sgz, rgz, sgx, rgx, sgc, rgc,
 ):
     NZ = DP // 2
@@ -53,7 +53,8 @@
     VC = VD // DP
     ROWS = DP * 8
     HALF = ROWS // 2
-    BW = gain.shape[1]
+    BW = owr.shape[2] - 64
+    WIN = owr.shape[2]
     LW = cv.shape[1]
     T = cv.shape[2]
     HEADS = q1v.shape[2]
@@ -77,14 +78,21 @@
     def local(src, dst, k):
         return pltpu.make_async_copy(src, dst, ld.at[k])
 
+    def window(e):
+        start = (e // 2) * 2 * BW + (e % 2) * (2 * BW - WIN)
+        return pl.ds(pl.multiple_of(start, 128), WIN)
+
+    pair_cols = pl.ds(pl.multiple_of((ep // 2) * 2 * BW, 128), 2 * BW)
+    group_rows = pl.ds(pl.multiple_of((dp // 4) * 16, 16), 16)
     loads = [local(q_h.at[1], q2v, 0), local(q_h.at[0], q1v, 1)]
     loads += [local(cache_h.at[s], cv.at[s], 2 + s) for s in range(SL)]
     loads += [
         local(vw_h, vw, 6),
-        local(ow_h, ow, 7),
+        local(resid.at[:, group_rows, pair_cols], rv, 7),
         local(gate_h, gu.at[:, pl.ds(0, 128)], 8),
         local(up_h, gu.at[:, pl.ds(128, 128)], 9),
-        local(down_h, dn, 10),
+        local(ow_h.at[:, window(ep)], owr.at[ep], 10),
+        local(down_h.at[:, window(ep)], dnr.at[ep], 11),
     ]
     for c in loads:
         c.start()
@@ -112,6 +120,25 @@
         return remote(a1s.at[mine], a1r.at[dp], sa1.at[d], ra1.at[dp], d, ep)
 
     loop(1, DP, lambda k: a1(k).start())
+
+    def ow_copy(i):
+        e = to_ep(i)
+        return remote(ow_h.at[:, window(e)], owr.at[ep], sow.at[e], row_.at[ep], dp, e)
+
+    def dn_copy(i):
+        e = to_ep(i)
+        return remote(down_h.at[:, window(e)], dnr.at[ep], sdn.at[e], rdn.at[ep], dp, e)
+
+    def ow_wait(i):
+        e = to_ep(i)
+        remote(ow_h.at[:, window(e)], owr.at[e], sow.at[e], row_.at[e], dp, e).wait_recv()
+
+    def dn_wait(i):
+        e = to_ep(i)
+        remote(down_h.at[:, window(e)], dnr.at[e], sdn.at[e], rdn.at[e], dp, e).wait_recv()
+
+    loop(1, EP, lambda i: ow_copy(i).start())
+    loop(1, EP // 2, lambda i: dn_copy(i).start())
 
     def attend(q, s, live_fresh):
         kt = cv[s]
@@ -216,6 +243,20 @@
         jnp.sum(jnp.where(own_place, weight, 0.0), axis=1, keepdims=True), (ROWS, 128)
     )
     place = jnp.where(place, 1.0, 0.0).astype(BF)
+    odd_block = ep % 2 == 1
+    lines = 2 * BW // 128
+    seven = jnp.zeros((lines, 128), F32)
+    for i in range(EP // 2):
+        seven = jnp.where(ep // 2 == i, gain[lines * i : lines * (i + 1)], seven)
+    seven = jnp.concatenate([seven[i : i + 1] for i in range(lines)], axis=1)
+    own_gain = jnp.where(odd_block, seven[:, BW:], seven[:, :BW])
+    loads[7].wait()
+    wide = rv[...].astype(F32)
+    own_resid = jnp.zeros((8, 2 * BW), F32)
+    for i in range(4):
+        rows = jnp.concatenate([wide[0, 4 * i : 4 * i + 4], wide[1, 4 * i : 4 * i + 4]], axis=0)
+        own_resid = jnp.where(dp % 4 == i, rows, own_resid)
+    own_resid = jnp.where(odd_block, own_resid[:, BW:], own_resid[:, :BW])
 
     loop(1, EP, a2_wait)
     moved_f = a2r[LW : LW + 16].astype(F32)
@@ -263,7 +304,7 @@
     loads[6].wait()
     merge(0)
     merge(1)
-    loads[7].wait()
+    loop(EP // 2, EP, lambda i: dn_copy(i).start())
 
     lanes = HP * VC
     pick = jnp.where(
@@ -279,85 +320,71 @@
         used.append(jnp.sum(picked.reshape(DP * SL, HP, lanes), axis=1))
     used = dot(place, jnp.concatenate(used, axis=0).astype(BF)).astype(BF)
 
+    def u_copy(i):
+        e = to_ep(i)
+        return remote(us, ur.at[ep], su.at[e], ru.at[ep], dp, e)
+
+    def u_wait(i):
+        e = to_ep(i)
+        remote(us, ur.at[e], su.at[e], ru.at[e], dp, e).wait_recv()
+
+    us[...] = used
+    ur[ep] = used
+    loop(1, EP, lambda i: u_copy(i).start())
+
     own_rows = pl.ds(pl.multiple_of(core * HALF, 16), HALF)
     other_rows = pl.ds(pl.multiple_of((1 - core) * HALF, 16), HALF)
     sibling = z * 2 + (1 - core)
-
-    def reduce_scatter(product, pc, pr, xs, xr, zs, zr, s_c, r_c, s_x, r_x, s_z, r_z):
-        def c_copy(j):
-            return remote(pc.at[j, other_rows], pr.at[j], s_c.at[j], r_c.at[j], sibling, ep)
-
-        def x_copy(j):
-            return remote(xs.at[j], xr.at[ep], s_x.at[j], r_x.at[ep], dp, j)
-
-        def z_copy(i):
-            t = (z + i) % NZ
-            return remote(zs.at[t], zr.at[z], s_z.at[t], r_z.at[z], t * 2 + core, ep)
-
-        def pair(i):
-            return (ep // 2 + 1 + i) % (EP // 2)
-
-        def first(i):
-            jp = pair(i)
-            part = product(pl.ds(pl.multiple_of(jp * 2 * BW, 128), 2 * BW))
-            pc[2 * jp] = part[:, :BW].astype(BF)
-            pc[2 * jp + 1] = part[:, BW:].astype(BF)
-            c_copy(2 * jp).start()
-            c_copy(2 * jp + 1).start()
-
-        loop(0, EP // 2, first)
-
-        def second(i):
-            for t in range(2):
-                j = 2 * pair(i) + t
-                c_copy(j).wait_recv()
-                part = (pc[j, own_rows].astype(F32) + pr[j].astype(F32)).astype(BF)
-                xs[j] = part
-
-                @pl.when(j != ep)
-                def _():
-                    x_copy(j).start()
-
-        loop(0, EP // 2, second)
-        xr[ep] = xs[ep]
-
-        def x_wait(i):
-            j = to_ep(i)
-            remote(xs.at[j], xr.at[j], s_x.at[j], r_x.at[j], dp, j).wait_recv()
-
-        loop(1, EP, x_wait)
-        total = lax.fori_loop(
-            0, EP, lambda j, acc: acc + xr[j].astype(F32), jnp.zeros((HALF, BW), F32)
+    my_block = core * NZ + z
+    odd = ep % 2 == 1
+    HB = BW // 2
+
+    def own_columns(part):
+        return jnp.where(odd, part[:, WIN - BW :], part[:, :BW])
+
+    def sum_over_dp(part, es, er, s_e, r_e):
+        part = part.reshape(DP, 8, BW)
+        es[...] = jnp.concatenate([part[:, :, :HB], part[:, :, HB:]], axis=1).astype(BF)
+        er[my_block] = es[my_block]
+
+        def e_copy(i):
+            d = to_dp(i)
+            b = (d % 2) * NZ + d // 2
+            return remote(es.at[b], er.at[my_block], s_e.at[b], r_e.at[my_block], d, ep)
+
+        def e_wait(i):
+            d = to_dp(i)
+            b = (d % 2) * NZ + d // 2
+            remote(es.at[b], er.at[b], s_e.at[b], r_e.at[b], d, ep).wait_recv()
+
+        loop(1, DP, lambda i: e_copy(i).start())
+        loop(1, DP, e_wait)
+        total = jnp.sum(er[...].astype(F32), axis=0)
+        return jnp.concatenate([total[:8], total[8:]], axis=1), lambda: loop(
+            1, DP, lambda i: e_copy(i).wait_send()
         )
-        zs[...] = total.reshape(NZ, 8, BW)
-        zr[z] = zs[z]
-        loop(1, NZ, lambda i: z_copy(i).start())
-
-        def z_wait(i):
-            t = (z + i) % NZ
-            remote(zs.at[t], zr.at[t], s_z.at[t], r_z.at[t], t * 2 + core, ep).wait_recv()
-
-        loop(1, NZ, z_wait)
-        result = jnp.sum(zr[...], axis=0)
-
-        def finish():
-            loop(0, EP, lambda j: c_copy(j).wait_send())
-            loop(1, EP, lambda i: x_copy(to_ep(i)).wait_send())
-            loop(1, NZ, lambda i: z_copy(i).wait_send())
-
-        return result, finish
-
-    attn, finish_one = reduce_scatter(
-        lambda cols: dot(used, ow[:, cols]),
-        pc, pr, xs, xr, zs, zr, s1c, r1c, s1x, r1x, s1z, r1z,
-    )
-    own_resid = jnp.concatenate([resid[0].astype(F32), resid[1].astype(F32)], axis=0)
+
+    loads[10].wait()
+    loop(1, EP, ow_wait)
+    loop(1, EP, u_wait)
+    every = jnp.concatenate([ur[e] for e in range(EP)], axis=1)
+    part = own_columns(dot(every, owr[...].reshape(EP * owr.shape[1], WIN)))
+    attn, finish_one = sum_over_dp(part, es1, er1, s1, r1)
     hidden = own_resid + attn
 
-    gs[:, :BW] = hidden * gain[...]
-    gs[:, BW:] = jnp.broadcast_to(
-        jnp.sum(hidden * hidden, axis=1, keepdims=True), (8, gs.shape[1] - BW)
-    )
+    scaled = hidden * own_gain
+    square = jnp.sum(hidden * hidden, axis=1, keepdims=True)
+    hi = square.astype(BF).astype(F32)
+    mid = (square - hi).astype(BF).astype(F32)
+    lane = iota((8, 256 - HB), 1)
+    extra = jnp.where(lane == 0, hi, jnp.where(lane == 1, mid, square - hi - mid))
+    gs[...] = jnp.concatenate(
+        [
+            jnp.concatenate([scaled[:, :HB], extra], axis=1),
+            jnp.concatenate([scaled[:, HB:], jnp.zeros_like(extra)], axis=1),
+        ],
+        axis=0,
+    ).astype(BF)
     gr[z] = gs[...]
 
     def gz_copy(i):
@@ -387,14 +414,10 @@
 
     loop(1, NZ, lambda i: gz_copy(i).start())
     loop(1, NZ, gz_wait)
-    wide = gr[...].reshape(HALF, gs.shape[1])
-    hi = wide.astype(BF).astype(F32)
-    mid = (wide - hi).astype(BF).astype(F32)
-    lo = wide - hi - mid
-    lane = iota(wide.shape, 1)
-    hb[ep, own_rows] = jnp.where(
-        lane <= BW, hi, jnp.where(lane == BW + 1, mid, lo)
-    ).astype(BF)
+    wide = gr[...].astype(F32)
+    top, low = wide[:, :8], wide[:, 8:]
+    wide = jnp.concatenate([top[:, :, :HB], low[:, :, :HB], top[:, :, HB:], low[:, :, HB:]], axis=2)
+    hb[ep, own_rows] = wide.reshape(HALF, 512).astype(BF)
     loop(1, EP, lambda i: gx_copy(i).start())
     gc_copy(ep).start()
     loads[8].wait()
@@ -425,13 +448,25 @@
     scale = lax.rsqrt(square / float(BW * EP) + NORM_EPS)
     g = proj[:, :128] * scale
     u = proj[:, 128:] * scale
-    act = (g / (1.0 + jnp.exp(-g)) * u).astype(BF)
-    loads[10].wait()
-    route = rw[:, 0:1]
-    routed, finish_two = reduce_scatter(
-        lambda cols: dot(act, dn[:, cols]) * route,
-        pc2, pr2, xs2, xr2, zs2, zr2, s2c, r2c, s2x, r2x, s2z, r2z,
-    )
+    act = (g / (1.0 + jnp.exp(-g)) * u * rw[:, 0:1]).astype(BF)
+    az[...] = act
+    ar[ep] = act
+
+    def act_copy(i):
+        e = to_ep(i)
+        return remote(az, ar.at[ep], sact.at[e], ract.at[ep], dp, e)
+
+    def act_wait(i):
+        e = to_ep(i)
+        remote(az, ar.at[e], sact.at[e], ract.at[e], dp, e).wait_recv()
+
+    loop(1, EP, lambda i: act_copy(i).start())
+    loads[11].wait()
+    loop(1, EP, dn_wait)
+    loop(1, EP, act_wait)
+    every = jnp.concatenate([ar[e] for e in range(EP)], axis=1)
+    part = own_columns(dot(every, dnr[...].reshape(EP * 128, WIN)))
+    routed, finish_two = sum_over_dp(part, es2, er2, s2, r2)
     mixed = (hidden + routed).astype(out.dtype)
     out[0] = mixed[0:4]
     out[1] = mixed[4:8]
@@ -447,6 +482,10 @@
     loop(1, EP, lambda i: gx_copy(i).wait_send())
     loop(0, EP, lambda e: gc_copy(e).wait_send())
     finish_two()
+    loop(1, EP, lambda i: ow_copy(i).wait_send())
+    loop(1, EP, lambda i: dn_copy(i).wait_send())
+    loop(1, EP, lambda i: u_copy(i).wait_send())
+    loop(1, EP, lambda i: act_copy(i).wait_send())
 
 
 def body(
@@ -463,41 +502,35 @@
     ROWS = DP * 8
     HALF = ROWS // 2
     PIECE = 768 // EP
-    dp = lax.axis_index("dp")
-    ep = lax.axis_index("ep")
     cache = jnp.swapaxes(latent_cache, 1, 2)
     q = jnp.swapaxes(queries, 2, 3)
-    gain = lax.dynamic_slice_in_dim(norm_gain, ep * BW, BW, 0).astype(F32).reshape(1, BW)
-    resid = lax.dynamic_slice(residual_stream, (0, dp * SL, ep * BW), (2, SL, BW))
+    gain = norm_gain.astype(F32).reshape(D // 128, 128)
     ow = output_weight.reshape(HP * output_weight.shape[1], D)
     smem = pl.BlockSpec(memory_space=pltpu.SMEM)
     vmem = pl.BlockSpec(memory_space=pltpu.VMEM)
     anyw = pl.BlockSpec(memory_space=pl.ANY)
     V = pltpu.VMEM
     sems = lambda *n: pltpu.SemaphoreType.DMA(n)
-    rs_bufs = [
-        V((EP, ROWS, BW), BF), V((EP, HALF, BW), BF), V((EP, HALF, BW), BF), V((EP, HALF, BW), BF),
-        V((NZ, 8, BW), F32), V((NZ, 8, BW), F32),
-    ]
-    rs_sems = [sems(EP), sems(EP), sems(EP), sems(EP), sems(NZ), sems(NZ)]
     scratch = [
-        V((SL, LW, H), BF), V((SL, LW, H), BF), V((SL, LW, T), BF), V(value_weight.shape, BF), V(ow.shape, BF),
-        V((D, 256), BF), V((128, D), BF),
+        V((SL, LW, H), BF), V((SL, LW, H), BF), V((SL, LW, T), BF), V(value_weight.shape, BF),
+        V((D, 256), BF), V((2, 16, 2 * BW), BF),
+        V((EP, ow.shape[0], BW + 64), BF), V((EP, 128, BW + 64), BF),
+        V((ROWS, ow.shape[0]), BF), V((EP, ROWS, ow.shape[0]), BF), V((ROWS, 128), BF), V((EP, ROWS, 128), BF),
         V((768, 128), BF), V((DP, PIECE, 128), BF), V((PIECE, 128), BF), V((768, 128), BF), V((16, LW), BF),
         V((2, EP, SL * HP, LAT), BF), V((2, EP, HP, 128), F32), V((2, EP, SL * HP, LAT), BF),
         V((2, EP, HP, 128), F32), V((EP, HP, 128), F32), V((SL * HP, LAT), BF),
         V((2, SL * HP, VD), BF), V((2, DP, SL * HP, VD), BF),
-        *rs_bufs, *rs_bufs,
-        V((8, 512), F32), V((NZ, 8, 512), F32), V((EP, ROWS, 512), BF), V((ROWS, 128), F32),
-        sems(11), sems(DP), sems(DP), sems(EP), sems(EP), sems(2, EP), sems(2, EP), sems(2, EP), sems(2, EP),
+        *[V((DP, 16, BW // 2), BF)] * 4,
+        V((16, 256), BF), V((NZ, 16, 256), BF), V((EP, ROWS, 512), BF), V((ROWS, 128), F32),
+        sems(12), sems(DP), sems(DP), sems(EP), sems(EP), sems(2, EP), sems(2, EP), sems(2, EP), sems(2, EP),
         sems(2, DP), sems(2, DP),
-        *rs_sems, *rs_sems,
+        *[sems(EP)] * 8, *[sems(DP)] * 4,
         sems(NZ), sems(NZ), sems(EP), sems(EP), sems(EP), sems(EP),
     ]
     return pl.pallas_call(
         functools.partial(kernel, DP, EP),
         out_shape=jax.ShapeDtypeStruct((2, SL, BW), BF),
-        in_specs=[smem] * 3 + [vmem] * 5 + [anyw] * 7,
+        in_specs=[smem] * 3 + [vmem] * 4 + [anyw] * 8,
         out_specs=vmem,
         scratch_shapes=scratch,
         compiler_params=pltpu.CompilerParams(
@@ -506,7 +539,7 @@
         name="decode",
     )(
         lengths, leaving, target, fresh_latent,
-        jnp.swapaxes(expert_ids, 1, 2), jnp.swapaxes(gate_codes, 1, 2), gain, resid,
+        jnp.swapaxes(expert_ids, 1, 2), jnp.swapaxes(gate_codes, 1, 2), gain, residual_stream,
         cache, q, value_weight, ow, gate_weight[0], up_weight[0], down_weight[0],
     )
 

time: 126 us -> 150 us (1.19)
  Pallas kernels: 123 us -> 147 us
    pallas_call x1, Pallas kernels: 123 us -> 147 us  [body(): pl.pallas_call(functools.partial(kernel, DP, EP), out_shape=jax.ShapeDtyp...]
where the time goes in v2:
time: 150 us
  Pallas kernels  147 us (98%)
    pallas_call x1, Pallas kernels, body(): pl.pallas_call(functools.partial(kernel, DP, EP), out_shape=jax.ShapeDtyp...  147 us

profile of v2, /device:TPU:1, one launch (start us, length us, event | category | flops | bytes accessed | tf_op | source)
XLA Modules:
  0.0 149.8 jit_solution(10867541102885557654)
XLA Ops:
  0.0 1.3 bitcast_convert_fusion.gain
  1.3 147.2 %decode.1 = bf16[2,4,448]{2,1,0:T(4,128)(2,1)} custom-call(s32[64]{0:T(128)} %lengths.1, s32[16]{0:T(128)} %leaving.1, s32[16]{0:T(128)} %target.1, bf16[2,4,576]{2,1,0:T(4,128)(2,1)} %fresh.1, s32[2,8,64]{2,1,0:T(8,128)} %bitcast.17, s32[2,8,64]{2,1,0:T(8,128)} %bitcast.18, f32[56,128]{1,0:T(8,128)} %bitcast_convert_fusion.gain, ...), custom_call_target="tpu_custom_call" | custom-call | tf_op jit(solution)/shard_map/decode/pallas_call | solution.py:530
  148.5 1.3 copy.17

commit v3 on v2

--- a/solution.py
+++ b/solution.py
@@ -29,21 +29,36 @@
     lax.fori_loop(lo, hi, lambda i, c: (fn(i), c)[1], 0)
 
 
+class Exchange:
+    def __init__(self, moves, lo, hi, copy, arrive):
+        self.lo, self.hi, self.copy, self.arrive = lo, hi, copy, arrive
+        moves.append(self)
+
+    def start(self):
+        loop(self.lo, self.hi, lambda i: self.copy(i).start())
+
+    def wait(self):
+        loop(self.lo, self.hi, lambda i: self.arrive(i).wait_recv())
+
+    def finish(self):
+        loop(self.lo, self.hi, lambda i: self.copy(i).wait_send())
+
+
 def kernel(
     DP, EP,
     lengths, leaving, target, fresh, ids, codes, gain, resid,
     cache_h, q_h, vw_h, ow_h, gate_h, up_h, down_h,
     out,
     q1v, q2v, cv, vw, gu, rv,
-    owr, dnr, us, ur, az, ar,
+    owr, us, ur, dn,
     a1s, a1r, a2s, a2r, fk,
     bs, bt, br, btr, sc, lat,
     cs, cr,
-    es1, er1, es2, er2,
+    es1, er1, pc, pr, xs, xr, zs, zr,
     gs, gr, hb, rw,
-    ld, sa1, ra1, sa2, ra2, sb, rb, st, rt, scs, rcs,
-    sow, row_, sdn, rdn, su, ru, sact, ract,
-    s1, r1, s2, r2,
+    ld, sa1, ra1, sa1c, ra1c, sa2, ra2, sb, rb, st, rt, scs, rcs,
+    sow, row_, su, ru, s1, r1,
+    s2c, r2c, s2x, r2x, s2z, r2z,
     sgz, rgz, sgx, rgx, sgc, rgc,
 ):
     NZ = DP // 2
@@ -63,6 +78,7 @@
     ep = lax.axis_index("ep")
     z = dp // 2
     core = dp % 2
+    sibling = z * 2 + (1 - core)
 
     def to_dp(k):
         return (dp + k) % DP
@@ -74,6 +90,30 @@
         return pltpu.make_async_remote_copy(
             src_ref=src, dst_ref=dst, send_sem=s, recv_sem=r, device_id=(d, e), device_id_type=MESH
         )
+
+    moves = []
+
+    def spread_dp(lo, hi, src, dst, s, r):
+        def copy(i):
+            d = to_dp(i)
+            return remote(src(d), dst(dp), s.at[d], r.at[dp], d, ep)
+
+        def arrive(i):
+            d = to_dp(DP - i)
+            return remote(src(d), dst(d), s.at[d], r.at[d], d, ep)
+
+        return Exchange(moves, lo, hi, copy, arrive)
+
+    def spread_ep(lo, hi, src, dst, s, r):
+        def copy(i):
+            e = to_ep(i)
+            return remote(src(e), dst(ep), s.at[e], r.at[ep], dp, e)
+
+        def arrive(i):
+            e = to_ep(EP - i)
+            return remote(src(e), dst(e), s.at[e], r.at[e], dp, e)
+
+        return Exchange(moves, lo, hi, copy, arrive)
 
     def local(src, dst, k):
         return pltpu.make_async_copy(src, dst, ld.at[k])
@@ -92,10 +132,9 @@
         local(gate_h, gu.at[:, pl.ds(0, 128)], 8),
         local(up_h, gu.at[:, pl.ds(128, 128)], 9),
         local(ow_h.at[:, window(ep)], owr.at[ep], 10),
-        local(down_h.at[:, window(ep)], dnr.at[ep], 11),
+        local(down_h, dn, 11),
     ]
-    for c in loads:
-        c.start()
+    loads[0].start()
 
     barrier = pltpu.get_barrier_semaphore()
     loop(1, DP, lambda k: pl.semaphore_signal(barrier, inc=1, device_id=(to_dp(k), ep), device_id_type=MESH))
@@ -112,40 +151,37 @@
     a1s[LW : LW + 16] = jnp.concatenate(fpieces + [jnp.zeros((11, 128), F32)], axis=0).astype(BF)
     a1s[LW + 16 :] = jnp.zeros((a1s.shape[0] - LW - 16, 128), BF)
     mine = pl.ds(pl.multiple_of(ep * PIECE, 16), PIECE)
-    a1r[dp] = a1s[mine]
+    a1r[core, z] = a1s[mine]
     pl.semaphore_wait(barrier, DP + EP - 2)
 
-    def a1(k):
-        d = to_dp(k)
-        return remote(a1s.at[mine], a1r.at[dp], sa1.at[d], ra1.at[dp], d, ep)
-
-    loop(1, DP, lambda k: a1(k).start())
-
-    def ow_copy(i):
-        e = to_ep(i)
-        return remote(ow_h.at[:, window(e)], owr.at[ep], sow.at[e], row_.at[ep], dp, e)
-
-    def dn_copy(i):
-        e = to_ep(i)
-        return remote(down_h.at[:, window(e)], dnr.at[ep], sdn.at[e], rdn.at[ep], dp, e)
-
-    def ow_wait(i):
-        e = to_ep(i)
-        remote(ow_h.at[:, window(e)], owr.at[e], sow.at[e], row_.at[e], dp, e).wait_recv()
-
-    def dn_wait(i):
-        e = to_ep(i)
-        remote(down_h.at[:, window(e)], dnr.at[e], sdn.at[e], rdn.at[e], dp, e).wait_recv()
-
-    loop(1, EP, lambda i: ow_copy(i).start())
-    loop(1, EP // 2, lambda i: dn_copy(i).start())
-
-    def attend(q, s, live_fresh):
+    def spread_z(src, dst, s, r):
+        def copy(i):
+            t = (z + i) % NZ
+            return remote(src(t), dst(z), s.at[t], r.at[z], t * 2 + core, ep)
+
+        def arrive(i):
+            t = (z + NZ - i) % NZ
+            return remote(src(t), dst(t), s.at[t], r.at[t], t * 2 + core, ep)
+
+        return Exchange(moves, 1, NZ, copy, arrive)
+
+    a1 = spread_z(lambda t: a1s.at[mine], lambda t: a1r.at[core, t], sa1, ra1)
+    a1.start()
+    for c in loads[1:]:
+        c.start()
+
+    def ow_from(e):
+        return ow_h.at[:, window(e)]
+
+    ow_x = spread_ep(1, EP // 2, ow_from, lambda e: owr.at[e], sow, row_)
+    ow_y = spread_ep(EP // 2, EP, ow_from, lambda e: owr.at[e], sow, row_)
+    ow_x.start()
+
+    def attend(q, s, live_fresh, fkeys):
         kt = cv[s]
         score = dot(q, kt, 0, 0) * SCORE_SCALE
         pos = ep * T + iota(score.shape, 1)
         live = pos < lengths[dp * SL + s]
-        fkeys = fk[...]
         fscore = dot(q, fkeys, 0, 1) * SCORE_SCALE
         score = jnp.where(live, score, MASKED)
         fscore = jnp.where(live_fresh, fscore, MASKED)
@@ -165,33 +201,23 @@
         for p in range(SL // 2):
             both = []
             for s in (2 * p, 2 * p + 1):
-                peak, total, v = attend(query_of(s), s, live_of(s))
+                peak, total, v = attend(query_of(s), s, live_of(s), fk[...])
                 stat = jnp.where(group == 2 * s, peak, jnp.where(group == 2 * s + 1, total, stat))
                 both.append(v.reshape(EP, HP, LAT))
             bs[k, :, 16 * p : 16 * p + 16, :] = jnp.concatenate(both, axis=1).astype(BF)
         bt[k] = stat.reshape(EP, HP, 128)
+
+    def keep_own(k):
         br[k, ep] = bs[k, ep]
         btr[k, ep] = bt[k, ep]
 
-    def b_copy(k, i):
-        e = to_ep(i)
-        return remote(bs.at[k, e], br.at[k, ep], sb.at[k, e], rb.at[k, ep], dp, e)
-
-    def t_copy(k, i):
-        e = to_ep(i)
-        return remote(bt.at[k, e], btr.at[k, ep], st.at[k, e], rt.at[k, ep], dp, e)
-
-    def b_wait(k, i):
-        e = to_ep(i)
-        remote(bs.at[k, e], br.at[k, e], sb.at[k, e], rb.at[k, e], dp, e).wait_recv()
-        remote(bt.at[k, e], btr.at[k, e], st.at[k, e], rt.at[k, e], dp, e).wait_recv()
-
-    def b_start(k):
-        def go(i):
-            t_copy(k, i).start()
-            b_copy(k, i).start()
-
-        loop(1, EP, go)
+    def partial_exchange(k):
+        return (
+            spread_ep(1, EP, lambda e: bt.at[k, e], lambda e: btr.at[k, e], st.at[k], rt.at[k]),
+            spread_ep(1, EP, lambda e: bs.at[k, e], lambda e: br.at[k, e], sb.at[k], rb.at[k]),
+        )
+
+    b_x = [partial_exchange(0), partial_exchange(1)]
 
     fcol = iota((1, 16), 1)
     at_zero = ep == 0
@@ -200,27 +226,28 @@
     for s in range(SL):
         loads[2 + s].wait()
     attend_step(0, lambda s: q1v[s], lambda s: (fcol == s) & at_zero)
-
-    def a1_wait(k):
-        d = to_dp(k)
-        remote(a1s.at[mine], a1r.at[d], sa1.at[d], ra1.at[d], d, ep).wait_recv()
-
-    loop(1, DP, a1_wait)
-    piece = a1r[target[dp]]
+    keep_own(0)
+
+    a1.wait()
+    a1c = Exchange(
+        moves, 0, 1,
+        lambda i: remote(a1r.at[core], a1r.at[core], sa1c, ra1c, sibling, ep),
+        lambda i: remote(a1r.at[1 - core], a1r.at[1 - core], sa1c, ra1c, sibling, ep),
+    )
+    a1c.start()
+    a1c.wait()
+    other = target[dp]
+    piece = a1r[other & 1, other >> 1]
     a2s[...] = piece
     a2r[mine] = piece
 
-    def a2(k):
-        e = to_ep(k)
-        return remote(a2s, a2r.at[mine], sa2.at[e], ra2.at[ep], dp, e)
-
-    def a2_wait(k):
-        e = to_ep(k)
-        rows = pl.ds(pl.multiple_of(e * PIECE, 16), PIECE)
-        remote(a2s, a2r.at[rows], sa2.at[e], ra2.at[e], dp, e).wait_recv()
-
-    loop(1, EP, lambda k: a2(k).start())
-    b_start(0)
+    def piece_rows(e):
+        return a2r.at[pl.ds(pl.multiple_of(e * PIECE, 16), PIECE)]
+
+    a2 = spread_ep(1, EP, lambda e: a2s, piece_rows, sa2, ra2)
+    a2.start()
+    for x in b_x[0]:
+        x.start()
 
     row = iota((ROWS, 2 * SL * DP), 0)
     col = iota((ROWS, 2 * SL * DP), 1)
@@ -258,30 +285,41 @@
         own_resid = jnp.where(dp % 4 == i, rows, own_resid)
     own_resid = jnp.where(odd_block, own_resid[:, BW:], own_resid[:, :BW])
 
-    loop(1, EP, a2_wait)
+    attend_step(1, lambda s: q2v[s], lambda s: ((fcol == s) | (fcol == 4 + s)) & at_zero)
+    a2.wait()
     moved_f = a2r[LW : LW + 16].astype(F32)
     moved_f = jnp.concatenate([moved_f[i : i + 1] for i in range(5)], axis=1)[:, :LW]
-    fk[...] = jnp.concatenate([f0, f1, moved_f, jnp.zeros((7, LW), F32)], axis=0).astype(BF)
-    moved_q = a2r[0:LW, 0:HEADS]
-    attend_step(
-        1,
-        lambda s: jnp.where(lv == s, moved_q, q2v[s]),
-        lambda s: ((fcol == s) | (fcol == jnp.where(lv == s, 8, 4 + s))) & at_zero,
+    fkeys = jnp.concatenate([f0, f1, moved_f, jnp.zeros((7, LW), F32)], axis=0).astype(BF)
+    peak, total, v = attend(
+        a2r[0:LW, 0:HEADS], lv, ((fcol == lv) | (fcol == 8)) & at_zero, fkeys
     )
-    b_start(1)
+    v = v.reshape(EP, HP, LAT)
+    twice = jnp.concatenate([v, v], axis=1)
+    upper = iota(twice.shape, 1) >> 3
+    for p in range(SL // 2):
+        rows = bs[1, :, 16 * p : 16 * p + 16, :].astype(F32)
+        bs[1, :, 16 * p : 16 * p + 16, :] = jnp.where(upper + 2 * p == lv, twice, rows).astype(BF)
+    stat = bt[1].reshape(HEADS, 128)
+    stat = jnp.where(group == 2 * lv, peak, jnp.where(group == 2 * lv + 1, total, stat))
+    bt[1] = stat.reshape(EP, HP, 128)
+    keep_own(1)
+    for x in b_x[1]:
+        x.start()
 
     head_of = iota((SL * HP, VD), 0) & (HP - 1)
 
-    def c_copy(k, i):
-        d = to_dp(i)
-        return remote(cs.at[k], cr.at[k, dp], scs.at[k, d], rcs.at[k, dp], d, ep)
-
-    def c_wait(k, i):
-        d = to_dp(i)
-        remote(cs.at[k], cr.at[k, d], scs.at[k, d], rcs.at[k, d], d, ep).wait_recv()
+    def value_exchange(k):
+        return spread_dp(
+            1, DP, lambda d: cs.at[k], lambda d: cr.at[k, d], scs.at[k], rcs.at[k]
+        )
+
+    c_x = [value_exchange(0), value_exchange(1)]
 
     def merge(k):
-        loop(1, EP, lambda i: b_wait(k, i))
+        for x in b_x[k]:
+            x.wait()
+        if k == 1:
+            ow_y.start()
         stats = btr[k]
         w = jnp.exp(stats - jnp.max(stats, axis=0, keepdims=True))
         shifted = jnp.concatenate([stats[:, :, 16:], stats[:, :, :16]], axis=2)
@@ -299,12 +337,11 @@
         values = values.astype(BF)
         cs[k] = values
         cr[k, dp] = values
-        loop(1, DP, lambda i: c_copy(k, i).start())
+        c_x[k].start()
 
     loads[6].wait()
     merge(0)
     merge(1)
-    loop(EP // 2, EP, lambda i: dn_copy(i).start())
 
     lanes = HP * VC
     pick = jnp.where(
@@ -314,27 +351,19 @@
     keep = (iota((DP * SL * HP, lanes), 0) & (HP - 1)) == (iota((DP * SL * HP, lanes), 1) >> vc_bits)
     used = []
     for k in range(2):
-        loop(1, DP, lambda i: c_wait(k, i))
+        c_x[k].wait()
         picked = dot(cr[k].reshape(DP * SL * HP, VD), pick)
         picked = jnp.where(keep, picked, 0.0)
         used.append(jnp.sum(picked.reshape(DP * SL, HP, lanes), axis=1))
     used = dot(place, jnp.concatenate(used, axis=0).astype(BF)).astype(BF)
 
-    def u_copy(i):
-        e = to_ep(i)
-        return remote(us, ur.at[ep], su.at[e], ru.at[ep], dp, e)
-
-    def u_wait(i):
-        e = to_ep(i)
-        remote(us, ur.at[e], su.at[e], ru.at[e], dp, e).wait_recv()
-
+    u_x = spread_ep(1, EP, lambda e: us, lambda e: ur.at[e], su, ru)
     us[...] = used
     ur[ep] = used
-    loop(1, EP, lambda i: u_copy(i).start())
+    u_x.start()
 
     own_rows = pl.ds(pl.multiple_of(core * HALF, 16), HALF)
     other_rows = pl.ds(pl.multiple_of((1 - core) * HALF, 16), HALF)
-    sibling = z * 2 + (1 - core)
     my_block = core * NZ + z
     odd = ep % 2 == 1
     HB = BW // 2
@@ -352,24 +381,24 @@
             b = (d % 2) * NZ + d // 2
             return remote(es.at[b], er.at[my_block], s_e.at[b], r_e.at[my_block], d, ep)
 
-        def e_wait(i):
+        def e_arrive(i):
             d = to_dp(i)
             b = (d % 2) * NZ + d // 2
-            remote(es.at[b], er.at[b], s_e.at[b], r_e.at[b], d, ep).wait_recv()
-
-        loop(1, DP, lambda i: e_copy(i).start())
-        loop(1, DP, e_wait)
+            return remote(es.at[b], er.at[b], s_e.at[b], r_e.at[b], d, ep)
+
+        x = Exchange(moves, 1, DP, e_copy, e_arrive)
+        x.start()
+        x.wait()
         total = jnp.sum(er[...].astype(F32), axis=0)
-        return jnp.concatenate([total[:8], total[8:]], axis=1), lambda: loop(
-            1, DP, lambda i: e_copy(i).wait_send()
-        )
+        return jnp.concatenate([total[:8], total[8:]], axis=1)
 
     loads[10].wait()
-    loop(1, EP, ow_wait)
-    loop(1, EP, u_wait)
+    ow_x.wait()
+    ow_y.wait()
+    u_x.wait()
     every = jnp.concatenate([ur[e] for e in range(EP)], axis=1)
     part = own_columns(dot(every, owr[...].reshape(EP * owr.shape[1], WIN)))
-    attn, finish_one = sum_over_dp(part, es1, er1, s1, r1)
+    attn = sum_over_dp(part, es1, er1, s1, r1)
     hidden = own_resid + attn
 
     scaled = hidden * own_gain
@@ -387,13 +416,7 @@
     ).astype(BF)
     gr[z] = gs[...]
 
-    def gz_copy(i):
-        t = (z + i) % NZ
-        return remote(gs, gr.at[z], sgz.at[t], rgz.at[z], t * 2 + core, ep)
-
-    def gz_wait(i):
-        t = (z + i) % NZ
-        remote(gs, gr.at[t], sgz.at[t], rgz.at[t], t * 2 + core, ep).wait_recv()
+    gz_x = spread_z(lambda t: gs, lambda t: gr.at[t], sgz, rgz)
 
     def gx_copy(i):
         e = to_ep(i)
@@ -412,8 +435,8 @@
         block = hb.at[e, other_rows]
         remote(block, block, sgc.at[e], rgc.at[e], sibling, ep).wait_recv()
 
-    loop(1, NZ, lambda i: gz_copy(i).start())
-    loop(1, NZ, gz_wait)
+    gz_x.start()
+    gz_x.wait()
     wide = gr[...].astype(F32)
     top, low = wide[:, :8], wide[:, 8:]
     wide = jnp.concatenate([top[:, :, :HB], low[:, :, :HB], top[:, :, HB:], low[:, :, HB:]], axis=2)
@@ -449,43 +472,67 @@
     g = proj[:, :128] * scale
     u = proj[:, 128:] * scale
     act = (g / (1.0 + jnp.exp(-g)) * u * rw[:, 0:1]).astype(BF)
-    az[...] = act
-    ar[ep] = act
-
-    def act_copy(i):
-        e = to_ep(i)
-        return remote(az, ar.at[ep], sact.at[e], ract.at[ep], dp, e)
-
-    def act_wait(i):
-        e = to_ep(i)
-        remote(az, ar.at[e], sact.at[e], ract.at[e], dp, e).wait_recv()
-
-    loop(1, EP, lambda i: act_copy(i).start())
     loads[11].wait()
-    loop(1, EP, dn_wait)
-    loop(1, EP, act_wait)
-    every = jnp.concatenate([ar[e] for e in range(EP)], axis=1)
-    part = own_columns(dot(every, dnr[...].reshape(EP * 128, WIN)))
-    routed, finish_two = sum_over_dp(part, es2, er2, s2, r2)
+
+    def c_copy(j):
+        return remote(pc.at[j, other_rows], pr.at[j], s2c.at[j], r2c.at[j], sibling, ep)
+
+    def x_copy(j):
+        return remote(xs.at[j], xr.at[ep], s2x.at[j], r2x.at[ep], dp, j)
+
+    def pair(i):
+        return (ep // 2 + 1 + i) % (EP // 2)
+
+    def first(i):
+        jp = pair(i)
+        part = dot(act, dn[:, pl.ds(pl.multiple_of(jp * 2 * BW, 128), 2 * BW)])
+        pc[2 * jp] = part[:, :BW].astype(BF)
+        pc[2 * jp + 1] = part[:, BW:].astype(BF)
+        c_copy(2 * jp).start()
+        c_copy(2 * jp + 1).start()
+
+    def second(i):
+        for t in range(2):
+            j = 2 * pair(i) + t
+            c_copy(j).wait_recv()
+            xs[j] = (pc[j, own_rows].astype(F32) + pr[j].astype(F32)).astype(BF)
+
+            @pl.when(j != ep)
+            def _():
+                x_copy(j).start()
+
+    def both(i):
+        first(i)
+        second(i - 1)
+
+    first(0)
+    loop(1, EP // 2, both)
+    second(EP // 2 - 1)
+
+    def x_sum(i, acc):
+        j = to_ep(EP - i)
+        remote(xs.at[j], xr.at[j], s2x.at[j], r2x.at[j], dp, j).wait_recv()
+        return acc + xr[j].astype(F32)
+
+    total = lax.fori_loop(1, EP, x_sum, xs[ep].astype(F32))
+    total = total.reshape(NZ, 8, BW)
+    zs[...] = jnp.concatenate([total[:, :, :HB], total[:, :, HB:]], axis=1).astype(BF)
+    zr[z] = zs[z]
+    z_x = spread_z(lambda t: zs.at[t], lambda t: zr.at[t], s2z, r2z)
+    z_x.start()
+    z_x.wait()
+    total = jnp.sum(zr[...].astype(F32), axis=0)
+    routed = jnp.concatenate([total[:8], total[8:]], axis=1)
     mixed = (hidden + routed).astype(out.dtype)
     out[0] = mixed[0:4]
     out[1] = mixed[4:8]
 
-    loop(1, DP, lambda k: a1(k).wait_send())
-    loop(1, EP, lambda k: a2(k).wait_send())
-    for k in range(2):
-        loop(1, EP, lambda i: b_copy(k, i).wait_send())
-        loop(1, EP, lambda i: t_copy(k, i).wait_send())
-        loop(1, DP, lambda i: c_copy(k, i).wait_send())
-    finish_one()
-    loop(1, NZ, lambda i: gz_copy(i).wait_send())
+    for x in moves:
+        x.finish()
     loop(1, EP, lambda i: gx_copy(i).wait_send())
     loop(0, EP, lambda e: gc_copy(e).wait_send())
-    finish_two()
-    loop(1, EP, lambda i: ow_copy(i).wait_send())
-    loop(1, EP, lambda i: dn_copy(i).wait_send())
-    loop(1, EP, lambda i: u_copy(i).wait_send())
-    loop(1, EP, lambda i: act_copy(i).wait_send())
+    loop(0, EP, lambda j: c_copy(j).wait_send())
+    loop(1, EP, lambda i: x_copy(to_ep(i)).wait_send())
 
 
 def body(
@@ -514,17 +561,18 @@
     scratch = [
         V((SL, LW, H), BF), V((SL, LW, H), BF), V((SL, LW, T), BF), V(value_weight.shape, BF),
         V((D, 256), BF), V((2, 16, 2 * BW), BF),
-        V((EP, ow.shape[0], BW + 64), BF), V((EP, 128, BW + 64), BF),
-        V((ROWS, ow.shape[0]), BF), V((EP, ROWS, ow.shape[0]), BF), V((ROWS, 128), BF), V((EP, ROWS, 128), BF),
-        V((768, 128), BF), V((DP, PIECE, 128), BF), V((PIECE, 128), BF), V((768, 128), BF), V((16, LW), BF),
+        V((EP, ow.shape[0], BW + 64), BF),
+        V((ROWS, ow.shape[0]), BF), V((EP, ROWS, ow.shape[0]), BF), V((128, D), BF),
+        V((768, 128), BF), V((2, NZ, PIECE, 128), BF), V((PIECE, 128), BF), V((768, 128), BF), V((16, LW), BF),
         V((2, EP, SL * HP, LAT), BF), V((2, EP, HP, 128), F32), V((2, EP, SL * HP, LAT), BF),
         V((2, EP, HP, 128), F32), V((EP, HP, 128), F32), V((SL * HP, LAT), BF),
         V((2, SL * HP, VD), BF), V((2, DP, SL * HP, VD), BF),
-        *[V((DP, 16, BW // 2), BF)] * 4,
+        *[V((DP, 16, BW // 2), BF)] * 2,
+        V((EP, ROWS, BW), BF), *[V((EP, HALF, BW), BF)] * 3, *[V((NZ, 16, BW // 2), BF)] * 2,
         V((16, 256), BF), V((NZ, 16, 256), BF), V((EP, ROWS, 512), BF), V((ROWS, 128), F32),
-        sems(12), sems(DP), sems(DP), sems(EP), sems(EP), sems(2, EP), sems(2, EP), sems(2, EP), sems(2, EP),
+        sems(12), sems(NZ), sems(NZ), pltpu.SemaphoreType.DMA, pltpu.SemaphoreType.DMA, sems(EP), sems(EP), sems(2, EP), sems(2, EP), sems(2, EP), sems(2, EP),
         sems(2, DP), sems(2, DP),
-        *[sems(EP)] * 8, *[sems(DP)] * 4,
+        *[sems(EP)] * 4, *[sems(DP)] * 2, *[sems(EP)] * 4, *[sems(NZ)] * 2,
         sems(NZ), sems(NZ), sems(EP), sems(EP), sems(EP), sems(EP),
     ]
     return pl.pallas_call(

time: 150 us -> 125 us (0.83)
  Pallas kernels: 147 us -> 121 us
    pallas_call x1, Pallas kernels: 147 us -> 121 us  [body(): pl.pallas_call(functools.partial(kernel, DP, EP), out_shape=jax.ShapeDtyp...]
where the time goes in v3:
time: 125 us; the launch traced here: 123 us
  Pallas kernels  121 us (97%)
  other arithmetic  1.31 us (1%)
  local copies, waits for them, and re-layouts  1.3 us (1%)
    pallas_call x1, Pallas kernels, body(): pl.pallas_call(functools.partial(kernel, DP, EP), out_shape=jax.ShapeDtyp...  121 us

profile of v3, /device:TPU:1, one launch (start us, length us, event | category | flops | bytes accessed | tf_op | source)
XLA Modules:
  0.0 123.5 jit_solution(17780592103866428179)
XLA Ops:
  0.0 1.3 %bitcast_convert_fusion.gain = f32[56,128]{1,0:T(8,128)} fusion(bf16[7168]{0:T(1024)(128)(2,1)} %param.24), kind=kLoop, calls=%fused_computation | loop fusion | flops 7168 | bytes 43008 | tf_op jit(solution)/shard_map/reshape | solution.py:554
  1.3 120.9 %decode.1 = bf16[2,4,448]{2,1,0:T(4,128)(2,1)} custom-call(s32[64]{0:T(128)} %lengths.1, s32[16]{0:T(128)} %leaving.1, s32[16]{0:T(128)} %target.1, bf16[2,4,576]{2,1,0:T(4,128)(2,1)} %fresh.1, s32[2,8,64]{2,1,0:T(8,128)} %bitcast.17, s32[2,8,64]{2,1,0:T(8,128)} %bitcast.18, f32[56,128]{1,0:T(8,128)} %bitcast_convert_fusion.gain, ...), custom_call_target="tpu_custom_call" | custom-call | tf_op jit(solution)/shard_map/decode/pallas_call | solution.py:578
  122.2 1.3 %copy.17 = bf16[2,4,448]{2,1,0:T(4,128)(2,1)} copy(bf16[2,4,448]{2,1,0:T(4,128)(2,1)} %decode.1) | data formatting | bytes 14336

commit v4 on v3

--- a/solution.py
+++ b/solution.py
@@ -50,14 +50,14 @@
     cache_h, q_h, vw_h, ow_h, gate_h, up_h, down_h,
     out,
     q1v, q2v, cv, vw, gu, rv,
-    owr, us, ur, dn,
+    owr, owp, vals, dn,
     a1s, a1r, a2s, a2r, fk,
     bs, bt, br, btr, sc, lat,
     cs, cr,
     es1, er1, pc, pr, xs, xr, zs, zr,
-    gs, gr, hb, rw,
+    gs, hb, rw,
     ld, sa1, ra1, sa1c, ra1c, sa2, ra2, sb, rb, st, rt, scs, rcs,
-    sow, row_, su, ru, s1, r1,
+    sow, row_, s1, r1,
     s2c, r2c, s2x, r2x, s2z, r2z,
     sgz, rgz, sgx, rgx, sgc, rgc,
 ):
@@ -70,6 +70,7 @@
     HALF = ROWS // 2
     BW = owr.shape[2] - 64
     WIN = owr.shape[2]
+    HB = BW // 2
     LW = cv.shape[1]
     T = cv.shape[2]
     HEADS = q1v.shape[2]
@@ -122,8 +123,11 @@
         start = (e // 2) * 2 * BW + (e % 2) * (2 * BW - WIN)
         return pl.ds(pl.multiple_of(start, 128), WIN)
 
-    pair_cols = pl.ds(pl.multiple_of((ep // 2) * 2 * BW, 128), 2 * BW)
-    group_rows = pl.ds(pl.multiple_of((dp // 4) * 16, 16), 16)
+    row_group = ep // 2
+    col_half = ep % 2
+    first_core, first_z = (2 * row_group) // NZ, (2 * row_group) % NZ
+    pair_cols = pl.ds(pl.multiple_of((dp // 2) * 2 * BW, 128), 2 * BW)
+    group_rows = pl.ds(pl.multiple_of(first_z * 8, 16), 16)
     loads = [local(q_h.at[1], q2v, 0), local(q_h.at[0], q1v, 1)]
     loads += [local(cache_h.at[s], cv.at[s], 2 + s) for s in range(SL)]
     loads += [
@@ -131,7 +135,7 @@
         local(resid.at[:, group_rows, pair_cols], rv, 7),
         local(gate_h, gu.at[:, pl.ds(0, 128)], 8),
         local(up_h, gu.at[:, pl.ds(128, 128)], 9),
-        local(ow_h.at[:, window(ep)], owr.at[ep], 10),
+        local(ow_h.at[:, window(dp)], owr.at[dp], 10),
         local(down_h, dn, 11),
     ]
     loads[0].start()
@@ -170,12 +174,7 @@
     for c in loads[1:]:
         c.start()
 
-    def ow_from(e):
-        return ow_h.at[:, window(e)]
-
-    ow_x = spread_ep(1, EP // 2, ow_from, lambda e: owr.at[e], sow, row_)
-    ow_y = spread_ep(EP // 2, EP, ow_from, lambda e: owr.at[e], sow, row_)
-    ow_x.start()
+    ow_x = spread_dp(1, DP, lambda d: ow_h.at[:, window(d)], lambda d: owr.at[d], sow, row_)
 
     def attend(q, s, live_fresh, fkeys):
         kt = cv[s]
@@ -236,6 +235,7 @@
     )
     a1c.start()
     a1c.wait()
+    ow_x.start()
     other = target[dp]
     piece = a1r[other & 1, other >> 1]
     a2s[...] = piece
@@ -260,7 +260,8 @@
     for r in range(DP):
         t = target[r]
         held = jnp.where(slot == t * SL + leaving[t], r * SL + leaving[r], held)
-    place = (r_step * (SL * DP) + jnp.where(r_step == 1, held, slot)) == col
+    held = jnp.where(r_step == 1, held, slot)
+    place = ((held >> 2) * 8 + r_step * 4 + (held & 3)) == col
     code = codes[...].astype(F32)
     share = code / jnp.sum(code, axis=1, keepdims=True) * ROUTE_SCALE
     weight = jnp.sum(jnp.where(ids[...] == ep, share, 0.0), axis=1)
@@ -270,20 +271,31 @@
         jnp.sum(jnp.where(own_place, weight, 0.0), axis=1, keepdims=True), (ROWS, 128)
     )
     place = jnp.where(place, 1.0, 0.0).astype(BF)
-    odd_block = ep % 2 == 1
     lines = 2 * BW // 128
     seven = jnp.zeros((lines, 128), F32)
+    mixed_gain = jnp.zeros((lines, 128), F32)
     for i in range(EP // 2):
-        seven = jnp.where(ep // 2 == i, gain[lines * i : lines * (i + 1)], seven)
+        seven = jnp.where(dp // 2 == i, gain[lines * i : lines * (i + 1)], seven)
+        mixed_gain = jnp.where(ep // 2 == i, gain[lines * i : lines * (i + 1)], mixed_gain)
     seven = jnp.concatenate([seven[i : i + 1] for i in range(lines)], axis=1)
-    own_gain = jnp.where(odd_block, seven[:, BW:], seven[:, :BW])
+    mixed_gain = jnp.concatenate([mixed_gain[i : i + 1] for i in range(lines)], axis=1)
+    mixed_gain = jnp.where(ep % 2 == 1, mixed_gain[:, BW:], mixed_gain[:, :BW])
+
+    def quarter(wide):
+        out = wide[:, :HB]
+        for i in range(1, 4):
+            out = jnp.where((dp % 2) * 2 + col_half == i, wide[:, HB * i : HB * (i + 1)], out)
+        return out
+
+    own_gain = quarter(seven)
     loads[7].wait()
     wide = rv[...].astype(F32)
-    own_resid = jnp.zeros((8, 2 * BW), F32)
-    for i in range(4):
-        rows = jnp.concatenate([wide[0, 4 * i : 4 * i + 4], wide[1, 4 * i : 4 * i + 4]], axis=0)
-        own_resid = jnp.where(dp % 4 == i, rows, own_resid)
-    own_resid = jnp.where(odd_block, own_resid[:, BW:], own_resid[:, :BW])
+    own_resid = [
+        jnp.where(first_core == 0, wide[k, 8 * t : 8 * t + 4], wide[k, 8 * t + 4 : 8 * t + 8])
+        for t in range(2)
+        for k in range(2)
+    ]
+    own_resid = quarter(jnp.concatenate(own_resid, axis=0))
 
     attend_step(1, lambda s: q2v[s], lambda s: ((fcol == s) | (fcol == 4 + s)) & at_zero)
     a2.wait()
@@ -308,18 +320,11 @@
 
     head_of = iota((SL * HP, VD), 0) & (HP - 1)
 
-    def value_exchange(k):
-        return spread_dp(
-            1, DP, lambda d: cs.at[k], lambda d: cr.at[k, d], scs.at[k], rcs.at[k]
-        )
-
-    c_x = [value_exchange(0), value_exchange(1)]
+    c_x = spread_dp(1, DP, lambda d: cs, lambda d: cr.at[d], scs, rcs)
 
     def merge(k):
         for x in b_x[k]:
             x.wait()
-        if k == 1:
-            ow_y.start()
         stats = btr[k]
         w = jnp.exp(stats - jnp.max(stats, axis=0, keepdims=True))
         shifted = jnp.concatenate([stats[:, :, 16:], stats[:, :, :16]], axis=2)
@@ -335,138 +340,120 @@
         for h in range(HP):
             values = jnp.where(head_of == h, dot(latent, vw[h]), values)
         values = values.astype(BF)
-        cs[k] = values
-        cr[k, dp] = values
-        c_x[k].start()
+        vals[SL * HP * k : SL * HP * (k + 1)] = values
 
     loads[6].wait()
     merge(0)
     merge(1)
 
-    lanes = HP * VC
-    pick = jnp.where(
-        iota((VD, lanes), 0) == dp * VC + (iota((VD, lanes), 1) & (VC - 1)), 1.0, 0.0
+    together = vals[...]
+    flat = []
+    for h in range(HP):
+        want = (iota((8, 2 * SL * HP), 0) >> 2) * (SL * HP) + (iota((8, 2 * SL * HP), 0) & 3) * HP + h
+        chosen = jnp.where(iota((8, 2 * SL * HP), 1) == want, 1.0, 0.0).astype(BF)
+        flat.append(dot(chosen, together))
+    half = HP // 2
+    flat = jnp.concatenate(
+        [jnp.concatenate(flat[:half], axis=1), jnp.concatenate(flat[half:], axis=1)], axis=0
     ).astype(BF)
-    vc_bits = VC.bit_length() - 1
-    keep = (iota((DP * SL * HP, lanes), 0) & (HP - 1)) == (iota((DP * SL * HP, lanes), 1) >> vc_bits)
-    used = []
-    for k in range(2):
-        c_x[k].wait()
-        picked = dot(cr[k].reshape(DP * SL * HP, VD), pick)
-        picked = jnp.where(keep, picked, 0.0)
-        used.append(jnp.sum(picked.reshape(DP * SL, HP, lanes), axis=1))
-    used = dot(place, jnp.concatenate(used, axis=0).astype(BF)).astype(BF)
-
-    u_x = spread_ep(1, EP, lambda e: us, lambda e: ur.at[e], su, ru)
-    us[...] = used
-    ur[ep] = used
-    u_x.start()
+    cs[...] = flat
+    cr[dp] = flat
+    c_x.start()
+
+    loads[10].wait()
+    ow_x.wait()
+    for h in range(HP):
+        lines_of = [owr[d, VC * h : VC * (h + 1)].astype(F32) for d in range(DP)]
+        owp[VD * h : VD * (h + 1)] = jnp.concatenate(lines_of, axis=0).astype(BF)
 
     own_rows = pl.ds(pl.multiple_of(core * HALF, 16), HALF)
     other_rows = pl.ds(pl.multiple_of((1 - core) * HALF, 16), HALF)
-    my_block = core * NZ + z
-    odd = ep % 2 == 1
-    HB = BW // 2
+    odd = dp % 2 == 1
 
     def own_columns(part):
         return jnp.where(odd, part[:, WIN - BW :], part[:, :BW])
 
-    def sum_over_dp(part, es, er, s_e, r_e):
-        part = part.reshape(DP, 8, BW)
-        es[...] = jnp.concatenate([part[:, :, :HB], part[:, :, HB:]], axis=1).astype(BF)
-        er[my_block] = es[my_block]
-
-        def e_copy(i):
-            d = to_dp(i)
-            b = (d % 2) * NZ + d // 2
-            return remote(es.at[b], er.at[my_block], s_e.at[b], r_e.at[my_block], d, ep)
-
-        def e_arrive(i):
-            d = to_dp(i)
-            b = (d % 2) * NZ + d // 2
-            return remote(es.at[b], er.at[b], s_e.at[b], r_e.at[b], d, ep)
-
-        x = Exchange(moves, 1, DP, e_copy, e_arrive)
-        x.start()
-        x.wait()
-        total = jnp.sum(er[...].astype(F32), axis=0)
-        return jnp.concatenate([total[:8], total[8:]], axis=1)
-
-    loads[10].wait()
-    ow_x.wait()
-    ow_y.wait()
-    u_x.wait()
-    every = jnp.concatenate([ur[e] for e in range(EP)], axis=1)
-    part = own_columns(dot(every, owr[...].reshape(EP * owr.shape[1], WIN)))
-    attn = sum_over_dp(part, es1, er1, s1, r1)
-    hidden = own_resid + attn
+    c_x.wait()
+    came = cr[...].astype(F32)
+    came = jnp.concatenate([came[:, :8], came[:, 8:]], axis=2).reshape(ROWS, HP * VD)
+    came = dot(place, came.astype(BF)).astype(BF)
+    part = own_columns(dot(came, owp[...])).astype(BF)
+    for g in range(EP // 2):
+        for t in range(2):
+            es1[2 * g + t] = part[16 * g : 16 * (g + 1), HB * t : HB * (t + 1)]
+    er1[ep] = es1[ep]
+    e_x = spread_ep(1, EP, lambda e: es1.at[e], lambda e: er1.at[e], s1, r1)
+    e_x.start()
+    e_x.wait()
+    hidden = own_resid + jnp.sum(er1[...].astype(F32), axis=0)
 
     scaled = hidden * own_gain
     square = jnp.sum(hidden * hidden, axis=1, keepdims=True)
     hi = square.astype(BF).astype(F32)
     mid = (square - hi).astype(BF).astype(F32)
-    lane = iota((8, 256 - HB), 1)
+    lane = iota((16, 256 - HB), 1)
     extra = jnp.where(lane == 0, hi, jnp.where(lane == 1, mid, square - hi - mid))
-    gs[...] = jnp.concatenate(
-        [
-            jnp.concatenate([scaled[:, :HB], extra], axis=1),
-            jnp.concatenate([scaled[:, HB:], jnp.zeros_like(extra)], axis=1),
-        ],
-        axis=0,
-    ).astype(BF)
-    gr[z] = gs[...]
-
-    gz_x = spread_z(lambda t: gs, lambda t: gr.at[t], sgz, rgz)
-
-    def gx_copy(i):
-        e = to_ep(i)
-        block = hb.at[ep, own_rows]
-        return remote(block, block, sgx.at[e], rgx.at[ep], dp, e)
-
-    def gx_wait(e):
-        block = hb.at[e, own_rows]
-        remote(block, block, sgx.at[e], rgx.at[e], dp, e).wait_recv()
-
-    def gc_copy(e):
-        block = hb.at[e, own_rows]
-        return remote(block, block, sgc.at[e], rgc.at[e], sibling, ep)
-
-    def gc_wait(e):
-        block = hb.at[e, other_rows]
-        remote(block, block, sgc.at[e], rgc.at[e], sibling, ep).wait_recv()
-
+    block = jnp.concatenate([scaled, extra], axis=1).astype(BF)
+    gs[...] = block
+
+    def rows_of(e):
+        return pl.ds(pl.multiple_of((e // 2) * 16, 16), 16)
+
+    hb[core, col_half, z, rows_of(ep)] = block
+    gz_x = spread_z(lambda t: gs, lambda t: hb.at[core, col_half, t, rows_of(ep)], sgz, rgz)
     gz_x.start()
     gz_x.wait()
-    wide = gr[...].astype(F32)
-    top, low = wide[:, :8], wide[:, 8:]
-    wide = jnp.concatenate([top[:, :, :HB], low[:, :, :HB], top[:, :, HB:], low[:, :, HB:]], axis=2)
-    hb[ep, own_rows] = wide.reshape(HALF, 512).astype(BF)
-    loop(1, EP, lambda i: gx_copy(i).start())
+
+    def region(e, c):
+        return hb.at[c, e % 2, :, rows_of(e)]
+
+    gx_x = Exchange(
+        moves, 1, EP,
+        lambda i: remote(
+            region(ep, core), region(ep, core), sgx.at[to_ep(i)], rgx.at[ep], dp, to_ep(i)
+        ),
+        lambda i: remote(
+            region(ep, core), region(to_ep(EP - i), core), sgx.at[ep], rgx.at[to_ep(EP - i)], dp, ep
+        ),
+    )
+
+    def gc_copy(e):
+        return remote(region(e, core), region(e, core), sgc.at[e], rgc.at[e], sibling, ep)
+
+    def gc_wait(e):
+        other = region(e, 1 - core)
+        remote(other, other, sgc.at[e], rgc.at[e], sibling, ep).wait_recv()
+
+    gx_x.start()
     gc_copy(ep).start()
     loads[8].wait()
     loads[9].wait()
 
-    def project(e, acc):
+    def pass_on(i):
+        gx_x.arrive(i).wait_recv()
+        gc_copy(to_ep(EP - i)).start()
+
+    loop(1, EP, pass_on)
+
+    def project(t, acc):
         proj, squares = acc
-        block = hb[e]
-        w = gu[pl.ds(pl.multiple_of(e * BW, 16), BW), :]
-        tail = block[:, 384:].astype(F32)
-        return proj + dot(block[:, :BW], w), squares + tail
-
-    def step(i, acc):
-        e = (ep + EP - i) % EP
-        gx_wait(e)
-        gc_copy(e).start()
-        before = (ep + EP - i + 1) % EP
-        gc_wait(before)
-        return project(before, acc)
-
+        for c in range(2):
+            for half in range(2):
+                block = hb[c, half, t]
+                w = gu[pl.ds(pl.multiple_of((2 * t + c) * BW + half * HB, 16), HB), :]
+                proj = proj + dot(block[:, :HB], w)
+                squares = squares + block[:, 128:].astype(F32)
+        return proj, squares
+
+    loop(0, EP, gc_wait)
     acc = (jnp.zeros((ROWS, 256), F32), jnp.zeros((ROWS, 128), F32))
-    acc = lax.fori_loop(1, EP, step, acc)
-    last = (ep + 1) % EP
-    gc_wait(last)
-    proj, squares = project(last, acc)
-    off = BW - 384
+    proj, squares = lax.fori_loop(0, NZ, project, acc)
+    at = pl.ds(pl.multiple_of((core * NZ + z) // 2 * 16, 16), 16)
+    sixteen = jnp.concatenate(
+        [hb[ep % 2, t, ep // 2, at, :].astype(F32)[:, :HB] for t in range(2)], axis=1
+    )
+    hidden = jnp.where(z % 2 == 1, sixteen[8:], sixteen[:8]) / mixed_gain
+    off = HB - 128
     square = squares[:, off : off + 1] + squares[:, off + 1 : off + 2] + squares[:, off + 2 : off + 3]
     scale = lax.rsqrt(square / float(BW * EP) + NORM_EPS)
     g = proj[:, :128] * scale
@@ -529,7 +516,6 @@
 
     for x in moves:
         x.finish()
-    loop(1, EP, lambda i: gx_copy(i).wait_send())
     loop(0, EP, lambda e: gc_copy(e).wait_send())
     loop(0, EP, lambda j: c_copy(j).wait_send())
     loop(1, EP, lambda i: x_copy(to_ep(i)).wait_send())
@@ -561,18 +547,18 @@
     scratch = [
         V((SL, LW, H), BF), V((SL, LW, H), BF), V((SL, LW, T), BF), V(value_weight.shape, BF),
         V((D, 256), BF), V((2, 16, 2 * BW), BF),
-        V((EP, ow.shape[0], BW + 64), BF),
-        V((ROWS, ow.shape[0]), BF), V((EP, ROWS, ow.shape[0]), BF), V((128, D), BF),
+        V((DP, ow.shape[0], BW + 64), BF),
+        V((HP * VD, BW + 64), BF), V((2 * SL * HP, VD), BF), V((128, D), BF),
         V((768, 128), BF), V((2, NZ, PIECE, 128), BF), V((PIECE, 128), BF), V((768, 128), BF), V((16, LW), BF),
         V((2, EP, SL * HP, LAT), BF), V((2, EP, HP, 128), F32), V((2, EP, SL * HP, LAT), BF),
         V((2, EP, HP, 128), F32), V((EP, HP, 128), F32), V((SL * HP, LAT), BF),
-        V((2, SL * HP, VD), BF), V((2, DP, SL * HP, VD), BF),
-        *[V((DP, 16, BW // 2), BF)] * 2,
+        V((16, HP * VD // 2), BF), V((DP, 16, HP * VD // 2), BF),
+        *[V((EP, 16, BW // 2), BF)] * 2,
         V((EP, ROWS, BW), BF), *[V((EP, HALF, BW), BF)] * 3, *[V((NZ, 16, BW // 2), BF)] * 2,
-        V((16, 256), BF), V((NZ, 16, 256), BF), V((EP, ROWS, 512), BF), V((ROWS, 128), F32),
+        V((16, 256), BF), V((2, 2, NZ, ROWS, 256), BF), V((ROWS, 128), F32),
         sems(12), sems(NZ), sems(NZ), pltpu.SemaphoreType.DMA, pltpu.SemaphoreType.DMA, sems(EP), sems(EP), sems(2, EP), sems(2, EP), sems(2, EP), sems(2, EP),
-        sems(2, DP), sems(2, DP),
-        *[sems(EP)] * 4, *[sems(DP)] * 2, *[sems(EP)] * 4, *[sems(NZ)] * 2,
+        sems(DP), sems(DP),
+        sems(DP), sems(DP), *[sems(EP)] * 2, *[sems(EP)] * 4, *[sems(NZ)] * 2,
         sems(NZ), sems(NZ), sems(EP), sems(EP), sems(EP), sems(EP),
     ]
     return pl.pallas_call(

time: 125 us -> 108 us (0.86)
  Pallas kernels: 121 us -> 104 us
    pallas_call x1, Pallas kernels: 121 us -> 104 us  [body(): pl.pallas_call(functools.partial(kernel, DP, EP), out_shape=jax.ShapeDtyp...]
where the time goes in v4:
time: 108 us; the launch traced here: 107 us
  Pallas kernels  104 us (96%)
  other arithmetic  1.31 us (1%)
  local copies, waits for them, and re-layouts  1.3 us (1%)
    pallas_call x1, Pallas kernels, body(): pl.pallas_call(functools.partial(kernel, DP, EP), out_shape=jax.ShapeDtyp...  104 us

profile of v4, /device:TPU:1, one launch (start us, length us, event | category | flops | bytes accessed | tf_op | source)
XLA Modules:
  0.0 107.0 jit_solution(17335670326107560193)
XLA Ops:
  0.0 1.3 %bitcast_convert_fusion.gain = f32[56,128]{1,0:T(8,128)} fusion(bf16[7168]{0:T(1024)(128)(2,1)} %param.24), kind=kLoop, calls=%fused_computation | loop fusion | flops 7168 | bytes 43008 | tf_op jit(solution)/shard_map/reshape | solution.py:540
  1.3 104.4 %decode.1 = bf16[2,4,448]{2,1,0:T(4,128)(2,1)} custom-call(s32[64]{0:T(128)} %lengths.1, s32[16]{0:T(128)} %leaving.1, s32[16]{0:T(128)} %target.1, bf16[2,4,576]{2,1,0:T(4,128)(2,1)} %fresh.1, s32[2,8,64]{2,1,0:T(8,128)} %bitcast.17, s32[2,8,64]{2,1,0:T(8,128)} %bitcast.18, f32[56,128]{1,0:T(8,128)} %bitcast_convert_fusion.gain, ...), custom_call_target="tpu_custom_call" | custom-call | tf_op jit(solution)/shard_map/decode/pallas_call | solution.py:564
  105.7 1.3 %copy.17 = bf16[2,4,448]{2,1,0:T(4,128)(2,1)} copy(bf16[2,4,448]{2,1,0:T(4,128)(2,1)} %decode.1) | data formatting | bytes 14336

commit v5 on v4

--- a/solution.py
+++ b/solution.py
@@ -50,7 +50,7 @@
     cache_h, q_h, vw_h, ow_h, gate_h, up_h, down_h,
     out,
     q1v, q2v, cv, vw, gu, rv,
-    owr, owp, vals, dn,
+    owr, owp, dn,
     a1s, a1r, a2s, a2r, fk,
     bs, bt, br, btr, sc, lat,
     cs, cr,
@@ -59,12 +59,12 @@
     ld, sa1, ra1, sa1c, ra1c, sa2, ra2, sb, rb, st, rt, scs, rcs,
     sow, row_, s1, r1,
     s2c, r2c, s2x, r2x, s2z, r2z,
-    sgz, rgz, sgx, rgx, sgc, rgc,
+    sgz, rgz, sgx, rgx, sgc, rgc, sga, rga, sgb, rgb,
 ):
     NZ = DP // 2
     SL = 4
-    HP = vw.shape[0]
-    VD = vw.shape[2]
+    HP = vw.shape[0] * 2
+    VD = vw.shape[2] // 2
     VC = VD // DP
     ROWS = DP * 8
     HALF = ROWS // 2
@@ -131,7 +131,6 @@
     loads = [local(q_h.at[1], q2v, 0), local(q_h.at[0], q1v, 1)]
     loads += [local(cache_h.at[s], cv.at[s], 2 + s) for s in range(SL)]
     loads += [
-        local(vw_h, vw, 6),
         local(resid.at[:, group_rows, pair_cols], rv, 7),
         local(gate_h, gu.at[:, pl.ds(0, 128)], 8),
         local(up_h, gu.at[:, pl.ds(128, 128)], 9),
@@ -139,6 +138,9 @@
         local(down_h, dn, 11),
     ]
     loads[0].start()
+    pairs = [
+        local(vw_h.at[h], vw.at[h // 2, :, pl.ds((h % 2) * VD, VD)], 12 + h) for h in range(HP)
+    ]
 
     barrier = pltpu.get_barrier_semaphore()
     loop(1, DP, lambda k: pl.semaphore_signal(barrier, inc=1, device_id=(to_dp(k), ep), device_id_type=MESH))
@@ -171,7 +173,7 @@
 
     a1 = spread_z(lambda t: a1s.at[mine], lambda t: a1r.at[core, t], sa1, ra1)
     a1.start()
-    for c in loads[1:]:
+    for c in loads[1:6] + pairs + loads[6:]:
         c.start()
 
     ow_x = spread_dp(1, DP, lambda d: ow_h.at[:, window(d)], lambda d: owr.at[d], sow, row_)
@@ -288,7 +290,7 @@
         return out
 
     own_gain = quarter(seven)
-    loads[7].wait()
+    loads[6].wait()
     wide = rv[...].astype(F32)
     own_resid = [
         jnp.where(first_core == 0, wide[k, 8 * t : 8 * t + 4], wide[k, 8 * t + 4 : 8 * t + 8])
@@ -320,7 +322,10 @@
 
     head_of = iota((SL * HP, VD), 0) & (HP - 1)
 
-    c_x = spread_dp(1, DP, lambda d: cs, lambda d: cr.at[d], scs, rcs)
+    c_x = [
+        spread_dp(1, DP, lambda d, k=k: cs.at[k], lambda d, k=k: cr.at[k, d], scs.at[k], rcs.at[k])
+        for k in range(2)
+    ]
 
     def merge(k):
         for x in b_x[k]:
@@ -337,30 +342,28 @@
 
         latent = lax.fori_loop(0, EP, add, jnp.zeros((SL * HP, LAT), F32)).astype(BF)
         values = jnp.zeros((SL * HP, VD), F32)
+        for p in range(HP // 2):
+            two = dot(latent, vw[p])
+            values = jnp.where(head_of == 2 * p, two[:, :VD], values)
+            values = jnp.where(head_of == 2 * p + 1, two[:, VD:], values)
+        values = values.astype(BF)
+        flat = []
         for h in range(HP):
-            values = jnp.where(head_of == h, dot(latent, vw[h]), values)
-        values = values.astype(BF)
-        vals[SL * HP * k : SL * HP * (k + 1)] = values
-
-    loads[6].wait()
+            want = iota((SL, SL * HP), 0) * HP + h
+            flat.append(dot(jnp.where(iota((SL, SL * HP), 1) == want, 1.0, 0.0).astype(BF), values))
+        few = HP // 4
+        flat = [jnp.concatenate(flat[few * t : few * (t + 1)], axis=1) for t in range(4)]
+        flat = jnp.concatenate(flat, axis=0).astype(BF)
+        cs[k] = flat
+        cr[k, dp] = flat
+        c_x[k].start()
+
+    for c in pairs:
+        c.wait()
     merge(0)
     merge(1)
 
-    together = vals[...]
-    flat = []
-    for h in range(HP):
-        want = (iota((8, 2 * SL * HP), 0) >> 2) * (SL * HP) + (iota((8, 2 * SL * HP), 0) & 3) * HP + h
-        chosen = jnp.where(iota((8, 2 * SL * HP), 1) == want, 1.0, 0.0).astype(BF)
-        flat.append(dot(chosen, together))
-    half = HP // 2
-    flat = jnp.concatenate(
-        [jnp.concatenate(flat[:half], axis=1), jnp.concatenate(flat[half:], axis=1)], axis=0
-    ).astype(BF)
-    cs[...] = flat
-    cr[dp] = flat
-    c_x.start()
-
-    loads[10].wait()
+    loads[9].wait()
     ow_x.wait()
     for h in range(HP):
         lines_of = [owr[d, VC * h : VC * (h + 1)].astype(F32) for d in range(DP)]
@@ -373,9 +376,12 @@
     def own_columns(part):
         return jnp.where(odd, part[:, WIN - BW :], part[:, :BW])
 
-    c_x.wait()
-    came = cr[...].astype(F32)
-    came = jnp.concatenate([came[:, :8], came[:, 8:]], axis=2).reshape(ROWS, HP * VD)
+    came = []
+    for k in range(2):
+        c_x[k].wait()
+        one = cr[k].astype(F32)
+        came.append(jnp.concatenate([one[:, SL * t : SL * (t + 1)] for t in range(4)], axis=2))
+    came = jnp.concatenate(came, axis=1).reshape(ROWS, HP * VD)
     came = dot(place, came.astype(BF)).astype(BF)
     part = own_columns(dot(came, owp[...])).astype(BF)
     for g in range(EP // 2):
@@ -407,15 +413,34 @@
     def region(e, c):
         return hb.at[c, e % 2, :, rows_of(e)]
 
-    gx_x = Exchange(
-        moves, 1, EP,
-        lambda i: remote(
-            region(ep, core), region(ep, core), sgx.at[to_ep(i)], rgx.at[ep], dp, to_ep(i)
-        ),
-        lambda i: remote(
-            region(ep, core), region(to_ep(EP - i), core), sgx.at[ep], rgx.at[to_ep(EP - i)], dp, ep
-        ),
-    )
+    def region_half(e, h):
+        return hb.at[core, e % 2, pl.ds(h * (NZ // 2), NZ // 2), rows_of(e)]
+
+    NX = 4 if EP == 16 else 2
+    NY = EP // NX
+    y, x = ep // NX, ep % NX
+
+    def on_x(i):
+        return y * NX + (x + i) % NX
+
+    def on_y(i):
+        return ((y + i) % NY) * NX + x
+
+    def whole(e):
+        return remote(region(ep, core), region(ep, core), sgx.at[e], rgx.at[ep], dp, e)
+
+    def whole_wait(e):
+        remote(region(e, core), region(e, core), sgx.at[e], rgx.at[e], dp, e).wait_recv()
+
+    def first_on(i, j):
+        e = on_x(NX - i)
+        half = region_half(e, 0)
+        return remote(half, half, sga.at[i, j], rga.at[e], dp, on_y(j))
+
+    def second_on(i, j):
+        e = on_y(NY - i)
+        half = region_half(e, 1)
+        return remote(half, half, sgb.at[i, j], rgb.at[e], dp, on_x(j))
 
     def gc_copy(e):
         return remote(region(e, core), region(e, core), sgc.at[e], rgc.at[e], sibling, ep)
@@ -424,16 +449,35 @@
         other = region(e, 1 - core)
         remote(other, other, sgc.at[e], rgc.at[e], sibling, ep).wait_recv()
 
-    gx_x.start()
+    loop(1, NX, lambda i: whole(on_x(i)).start())
+    loop(1, NY, lambda i: whole(on_y(i)).start())
     gc_copy(ep).start()
+    loads[7].wait()
     loads[8].wait()
-    loads[9].wait()
-
-    def pass_on(i):
-        gx_x.arrive(i).wait_recv()
-        gc_copy(to_ep(EP - i)).start()
-
-    loop(1, EP, pass_on)
+
+    def pass_x(i):
+        whole_wait(on_x(NX - i))
+        loop(1, NY, lambda j: first_on(i, j).start())
+        gc_copy(on_x(NX - i)).start()
+
+    def pass_y(i):
+        whole_wait(on_y(NY - i))
+        loop(1, NX, lambda j: second_on(i, j).start())
+        gc_copy(on_y(NY - i)).start()
+
+    def across(n):
+        e = ((y + 1 + n // (NX - 1)) % NY) * NX + (x + 1 + n % (NX - 1)) % NX
+        first, second = region_half(e, 0), region_half(e, 1)
+        remote(first, first, sga.at[0, 0], rga.at[e], dp, e).wait_recv()
+        remote(second, second, sgb.at[0, 0], rgb.at[e], dp, e).wait_recv()
+        gc_copy(e).start()
+
+    for i in range(1, max(NX, NY)):
+        if i < NX:
+            pass_x(i)
+        if i < NY:
+            pass_y(i)
+    loop(0, (NX - 1) * (NY - 1), across)
 
     def project(t, acc):
         proj, squares = acc
@@ -459,7 +503,7 @@
     g = proj[:, :128] * scale
     u = proj[:, 128:] * scale
     act = (g / (1.0 + jnp.exp(-g)) * u * rw[:, 0:1]).astype(BF)
-    loads[11].wait()
+    loads[10].wait()
 
     def c_copy(j):
         return remote(pc.at[j, other_rows], pr.at[j], s2c.at[j], r2c.at[j], sibling, ep)
@@ -482,7 +526,11 @@
         for t in range(2):
             j = 2 * pair(i) + t
             c_copy(j).wait_recv()
-            xs[j] = (pc[j, own_rows].astype(F32) + pr[j].astype(F32)).astype(BF)
+            part = pc[j, own_rows].astype(F32) + pr[j].astype(F32)
+            tail = part[:, BW - 64 :]
+            tail = jnp.concatenate([tail[: HALF // 2], tail[HALF // 2 :]], axis=1)
+            tiles = [part[:, 128 * i : 128 * (i + 1)] for i in range(BW // 128)]
+            xs[j] = jnp.concatenate(tiles + [tail], axis=0).astype(BF)
 
             @pl.when(j != ep)
             def _():
@@ -502,7 +550,10 @@
         return acc + xr[j].astype(F32)
 
     total = lax.fori_loop(1, EP, x_sum, xs[ep].astype(F32))
-    total = total.reshape(NZ, 8, BW)
+    tail = total[HALF * (BW // 128) :]
+    tail = jnp.concatenate([tail[:, :64], tail[:, 64:]], axis=0)
+    tiles = [total[HALF * i : HALF * (i + 1)] for i in range(BW // 128)]
+    total = jnp.concatenate(tiles + [tail], axis=1).reshape(NZ, 8, BW)
     zs[...] = jnp.concatenate([total[:, :, :HB], total[:, :, HB:]], axis=1).astype(BF)
     zr[z] = zs[z]
     z_x = spread_z(lambda t: zs.at[t], lambda t: zr.at[t], s2z, r2z)
@@ -514,8 +565,14 @@
     out[0] = mixed[0:4]
     out[1] = mixed[4:8]
 
-    for x in moves:
-        x.finish()
+    for move in moves:
+        move.finish()
+    loop(1, NX, lambda i: whole(on_x(i)).wait_send())
+    loop(1, NY, lambda i: whole(on_y(i)).wait_send())
+    for i in range(1, NX):
+        loop(1, NY, lambda j: first_on(i, j).wait_send())
+    for i in range(1, NY):
+        loop(1, NX, lambda j: second_on(i, j).wait_send())
     loop(0, EP, lambda e: gc_copy(e).wait_send())
     loop(0, EP, lambda j: c_copy(j).wait_send())
     loop(1, EP, lambda i: x_copy(to_ep(i)).wait_send())
@@ -545,21 +602,21 @@
     V = pltpu.VMEM
     sems = lambda *n: pltpu.SemaphoreType.DMA(n)
     scratch = [
-        V((SL, LW, H), BF), V((SL, LW, H), BF), V((SL, LW, T), BF), V(value_weight.shape, BF),
+        V((SL, LW, H), BF), V((SL, LW, H), BF), V((SL, LW, T), BF), V((HP // 2, value_weight.shape[1], 2 * VD), BF),
         V((D, 256), BF), V((2, 16, 2 * BW), BF),
         V((DP, ow.shape[0], BW + 64), BF),
-        V((HP * VD, BW + 64), BF), V((2 * SL * HP, VD), BF), V((128, D), BF),
+        V((HP * VD, BW + 64), BF), V((128, D), BF),
         V((768, 128), BF), V((2, NZ, PIECE, 128), BF), V((PIECE, 128), BF), V((768, 128), BF), V((16, LW), BF),
         V((2, EP, SL * HP, LAT), BF), V((2, EP, HP, 128), F32), V((2, EP, SL * HP, LAT), BF),
         V((2, EP, HP, 128), F32), V((EP, HP, 128), F32), V((SL * HP, LAT), BF),
-        V((16, HP * VD // 2), BF), V((DP, 16, HP * VD // 2), BF),
+        V((2, 16, HP * VD // 4), BF), V((2, DP, 16, HP * VD // 4), BF),
         *[V((EP, 16, BW // 2), BF)] * 2,
-        V((EP, ROWS, BW), BF), *[V((EP, HALF, BW), BF)] * 3, *[V((NZ, 16, BW // 2), BF)] * 2,
+        V((EP, ROWS, BW), BF), V((EP, HALF, BW), BF), *[V((EP, HALF * BW // 128, 128), BF)] * 2, *[V((NZ, 16, BW // 2), BF)] * 2,
         V((16, 256), BF), V((2, 2, NZ, ROWS, 256), BF), V((ROWS, 128), F32),
-        sems(12), sems(NZ), sems(NZ), pltpu.SemaphoreType.DMA, pltpu.SemaphoreType.DMA, sems(EP), sems(EP), sems(2, EP), sems(2, EP), sems(2, EP), sems(2, EP),
-        sems(DP), sems(DP),
+        sems(12 + HP), sems(NZ), sems(NZ), pltpu.SemaphoreType.DMA, pltpu.SemaphoreType.DMA, sems(EP), sems(EP), sems(2, EP), sems(2, EP), sems(2, EP), sems(2, EP),
+        sems(2, DP), sems(2, DP),
         sems(DP), sems(DP), *[sems(EP)] * 2, *[sems(EP)] * 4, *[sems(NZ)] * 2,
-        sems(NZ), sems(NZ), sems(EP), sems(EP), sems(EP), sems(EP),
+        sems(NZ), sems(NZ), sems(EP), sems(EP), sems(EP), sems(EP), sems(4, 4), sems(EP), sems(4, 4), sems(EP),
     ]
     return pl.pallas_call(
         functools.partial(kernel, DP, EP),

time: 108 us -> 106 us (0.981)
    pallas_call x1, Pallas kernels: 104 us -> 103 us  [body(): pl.pallas_call(functools.partial(kernel, DP, EP), out_shape=jax.ShapeDtyp...]
where the time goes in v5:
time: 106 us
  Pallas kernels  103 us (97%)
  other arithmetic  1.31 us (1%)
  local copies, waits for them, and re-layouts  1.3 us (1%)
    pallas_call x1, Pallas kernels, body(): pl.pallas_call(functools.partial(kernel, DP, EP), out_shape=jax.ShapeDtyp...  103 us

profile of v5, /device:TPU:1, one launch (start us, length us, event | category | flops | bytes accessed | tf_op | source)
XLA Modules:
  0.0 105.7 jit_solution(1767717755162079207)
XLA Ops:
  0.0 1.3 %bitcast_convert_fusion.gain = f32[56,128]{1,0:T(8,128)} fusion(bf16[7168]{0:T(1024)(128)(2,1)} %param.24), kind=kLoop, calls=%fused_computation | loop fusion | flops 7168 | bytes 43008 | tf_op jit(solution)/shard_map/reshape | solution.py:597
  1.3 103.1 %decode.1 = bf16[2,4,448]{2,1,0:T(4,128)(2,1)} custom-call(s32[64]{0:T(128)} %lengths.1, s32[16]{0:T(128)} %leaving.1, s32[16]{0:T(128)} %target.1, bf16[2,4,576]{2,1,0:T(4,128)(2,1)} %fresh.1, s32[2,8,64]{2,1,0:T(8,128)} %bitcast.17, s32[2,8,64]{2,1,0:T(8,128)} %bitcast.18, f32[56,128]{1,0:T(8,128)} %bitcast_convert_fusion.gain, ...), custom_call_target="tpu_custom_call" | custom-call | tf_op jit(solution)/shard_map/decode/pallas_call | solution.py:621
  104.4 1.3 %copy.17 = bf16[2,4,448]{2,1,0:T(4,128)(2,1)} copy(bf16[2,4,448]{2,1,0:T(4,128)(2,1)} %decode.1) | data formatting | bytes 14336

commit v6 on v5

--- a/solution.py
+++ b/solution.py
@@ -176,7 +176,13 @@
     for c in loads[1:6] + pairs + loads[6:]:
         c.start()
 
-    ow_x = spread_dp(1, DP, lambda d: ow_h.at[:, window(d)], lambda d: owr.at[d], sow, row_)
+    near = DP // 5
+    ow_x = [
+        spread_dp(lo, hi, lambda d: ow_h.at[:, window(d)], lambda d: owr.at[d], sow, row_)
+        for lo, hi in ((1, 1 + near), (DP - near, DP), (1 + near, DP - near))
+    ]
+    ow_x[0].start()
+    ow_x[1].start()
 
     def attend(q, s, live_fresh, fkeys):
         kt = cv[s]
@@ -237,7 +243,7 @@
     )
     a1c.start()
     a1c.wait()
-    ow_x.start()
+    ow_x[2].start()
     other = target[dp]
     piece = a1r[other & 1, other >> 1]
     a2s[...] = piece
@@ -364,7 +370,8 @@
     merge(1)
 
     loads[9].wait()
-    ow_x.wait()
+    for move in ow_x:
+        move.wait()
     for h in range(HP):
         lines_of = [owr[d, VC * h : VC * (h + 1)].astype(F32) for d in range(DP)]
         owp[VD * h : VD * (h + 1)] = jnp.concatenate(lines_of, axis=0).astype(BF)

time: 106 us -> 102 us (0.962)
  Pallas kernels: 103 us -> 98.9 us
    pallas_call x1, Pallas kernels: 103 us -> 98.9 us  [body(): pl.pallas_call(functools.partial(kernel, DP, EP), out_shape=jax.ShapeDtyp...]
where the time goes in v6:
time: 102 us
  Pallas kernels  98.9 us (97%)
  other arithmetic  1.31 us (1%)
  local copies, waits for them, and re-layouts  1.3 us (1%)
    pallas_call x1, Pallas kernels, body(): pl.pallas_call(functools.partial(kernel, DP, EP), out_shape=jax.ShapeDtyp...  98.9 us

profile of v6, /device:TPU:1, one launch (start us, length us, event | category | flops | bytes accessed | tf_op | source)
XLA Modules:
  0.0 101.5 jit_solution(12200251889038532314)
XLA Ops:
  0.0 1.3 %bitcast_convert_fusion.gain = f32[56,128]{1,0:T(8,128)} fusion(bf16[7168]{0:T(1024)(128)(2,1)} %param.24), kind=kLoop, calls=%fused_computation | loop fusion | flops 7168 | bytes 43008 | tf_op jit(solution)/shard_map/reshape | solution.py:604
  1.3 98.9 %decode.1 = bf16[2,4,448]{2,1,0:T(4,128)(2,1)} custom-call(s32[64]{0:T(128)} %lengths.1, s32[16]{0:T(128)} %leaving.1, s32[16]{0:T(128)} %target.1, bf16[2,4,576]{2,1,0:T(4,128)(2,1)} %fresh.1, s32[2,8,64]{2,1,0:T(8,128)} %bitcast.17, s32[2,8,64]{2,1,0:T(8,128)} %bitcast.18, f32[56,128]{1,0:T(8,128)} %bitcast_convert_fusion.gain, ...), custom_call_target="tpu_custom_call" | custom-call | tf_op jit(solution)/shard_map/decode/pallas_call | solution.py:628
  100.2 1.3 %copy.17 = bf16[2,4,448]{2,1,0:T(4,128)(2,1)} copy(bf16[2,4,448]{2,1,0:T(4,128)(2,1)} %decode.1) | data formatting | bytes 14336
